TPU v7x, 32 devices: a whole 2x2x4 slice. The times are simulated.
32 devices in a mesh: ctx: 8 (over z, x), tp: 4 (over y, core).
Axes of the slice: x: 2, y: 2, z: 4, core: 2. Of those that a mesh axis runs over, the one named last changes fastest.
Arguments:
- query: bfloat16 [1024, 8192], P('ctx', 'tp'), may hold values from -6 to 6
- keys: bfloat16 [1024, 8192], P('ctx', 'tp'), may hold values from -6 to 6
- values: bfloat16 [1024, 8192], P('ctx', 'tp'), may hold values from -6 to 6
- rates: float32 [16, 8192], P(None, 'tp'), may hold values from 0.00048828125 to 0.03
- residues: float32 [16, 8192], P(None, 'tp'), may hold values from -3 to 3
- skip: float32 [8192], P('tp'), may hold values from 0.25 to 1.5
- gain: float32 [8192], P('tp'), may hold values from 0.25 to 1.75
Outputs:
- mixed: bfloat16 [1024, 8192], P('ctx', 'tp')
All inputs are finite; a program needn't handle non-finite values.
Results may differ from a plain program's by a relative error of at most 0.0025.
Values sent between devices are 32-bit elements; how exact they have to be, the bound alone decides.
No kernel may reach another device: no remote copies, remote signals or barrier semaphores. Data moves between devices by JAX's collectives and lax.ppermute only.
A program may use at most 64 MiB of HBM per device.

v0:
```python
import jax
import jax.numpy as jnp
from jax import lax
from jax.sharding import PartitionSpec as P

C = 8192


def combine_pair(first, second):
    return (first[0] * second[0], first[1] * second[0] + second[1])


def body(query, keys, values, rates, residues, skip, gain):
    driven = keys.astype(jnp.float32) * values.astype(jnp.float32)
    count = driven.shape[0]

    def one_mode(total, mode):
        rate, residue = mode
        decay = jnp.exp(-rate)
        scale = residue * jnp.sqrt(1.0 - decay * decay)
        factors = jnp.broadcast_to(decay[None, :], driven.shape)
        state = lax.associative_scan(combine_pair, (factors, driven), axis=0)[1]
        return (total + scale[None, :] * state, state[count - 1])

    start = jnp.zeros(driven.shape, jnp.float32)
    local_part, end_states = lax.scan(one_mode, start, (rates, residues))
    own_index = lax.axis_index("ctx")
    piece = lax.all_gather(end_states[None], "ctx", axis=0, tiled=True)
    number = piece.shape[0]
    sources = jnp.arange(number, dtype=jnp.int32)
    before = sources < own_index
    gaps = jnp.maximum(own_index - 1 - sources, 0).astype(jnp.float32) * count
    weights = jnp.exp(-rates[None, :, :] * gaps[:, None, None])
    weights = jnp.where(before[:, None, None], weights, 0.0)
    carried = jnp.sum(weights * piece, axis=0)
    decay_all = jnp.exp(-rates)
    weighted = residues * jnp.sqrt(1.0 - decay_all * decay_all) * carried
    steps_ahead = jnp.arange(1, count + 1, dtype=jnp.float32)
    powers = jnp.exp(-rates[None, :, :] * steps_ahead[:, None, None])
    filtered = local_part + jnp.sum(powers * weighted[None, :, :], axis=1)
    gated = query.astype(jnp.float32) * (filtered + skip[None, :] * driven)
    partial_sq = jnp.sum(gated * gated, axis=1)
    total_sq = lax.psum(partial_sq, "tp")
    power = total_sq / C
    return (gated * lax.rsqrt(power + 1e-06)[:, None] * gain[None, :]).astype(jnp.bfloat16)


def solution(mesh):
    in_specs = (
        P("ctx", "tp"),
        P("ctx", "tp"),
        P("ctx", "tp"),
        P(None, "tp"),
        P(None, "tp"),
        P("tp"),
        P("tp"),
    )
    out_specs = P("ctx", "tp")
    return jax.shard_map(body, mesh=mesh, in_specs=in_specs, out_specs=out_specs, check_vma=False)
```

profile of v0, /device:TPU:0, one launch (start us, length us, event | category | flops | bytes accessed | tf_op | source)
XLA Modules:
  0.0 315.1 jit_solution(7394178761772627906)
XLA Ops:
  7.9 243.1 %while.13 = (s32[]{:T(128)}, f32[128,2048]{1,0:T(8,128)}, f32[16,2048]{1,0:T(8,128)}, f32[16,2048]{1,0:T(8,128)S(1)}, f32[16,2048]{1,0:T(8,128)S(1)}, /*index=5*...) while((s32[]{:T(128)}, f32[128,2048]{1,0:T(8,128)}, f32[16,2048]{1,0:T(8,128)}, ...), condition=%wide.region_1.2_spmd.clone, body=%wide.region_0.1_spmd.clone.sunk | while | flops 2865155 | bytes 29008028 | solution.py:26
  11.5 2.1 pad.147
  17.2 2.1 pad.146
  25.6 2.1 pad.147
  31.2 2.1 pad.146
  34.8 2.4 select_add_fusion.2
  40.8 2.1 pad.147
  46.5 2.1 pad.146
  50.1 2.4 select_add_fusion.2
  56.1 2.1 pad.147
  61.7 2.1 pad.146
  65.4 2.4 select_add_fusion.2
  71.4 2.1 pad.147
  80.6 2.4 select_add_fusion.2
  95.9 2.4 select_add_fusion.2
  111.2 2.4 select_add_fusion.2
  126.4 2.4 select_add_fusion.2
  141.7 2.4 select_add_fusion.2
  147.7 2.1 pad.147
  153.3 2.1 pad.146
  157.0 2.4 select_add_fusion.2
  172.2 2.4 select_add_fusion.2
  187.5 2.4 select_add_fusion.2
  199.2 2.1 pad.146
  202.8 2.4 select_add_fusion.2
  208.8 2.1 pad.147
  218.1 2.4 select_add_fusion.2
  233.3 2.4 select_add_fusion.2
  248.6 2.4 select_add_fusion.2
  251.1 42.9 %all-gather.3.cloned.1.call-done = f32[128,2048]{1,0:T(8,128)} async-done(((f32[16,2048]{1,0:T(8,128)}), f32[128,2048]{1,0:T(8,128)}) %all-gather.3.cloned.1.call-update) | async-done | bytes 1048592 | tf_op jit(solution)/shard_map/all_gather | solution.py:28
  295.7 5.3 %multiply_reduce_fusion = f32[128,2048]{1,0:T(8,128)S(1)} fusion(f32[16,2048]{1,0:T(8,128)S(1)} %multiply_multiply_fusion.4, f32[128]{0:T(128)S(1)} %iota_add_fusion, f32[16,2048]{1,0:T(8,128)S(1)} %neg.11), kind=kLoop, calls=%fused_computation.38 | loop fusion | flops 12320768 | bytes 1311232 | tf_op jit(solution)/shard_map/reduce_sum | solution.py:40
  301.6 5.7 %psum.7 = f32[128]{0:T(128)S(1)} all-reduce(f32[128]{0:T(128)S(1)} %get-tuple-element.75), channel_id=1, replica_groups=mesh['ctx'=8,'tp'=4] {'tp'}, use_global_device_ids=true, to_apply=%region_5.6 | all-reduce | flops 128 | bytes 1024 | tf_op jit(solution)/shard_map/psum | solution.py:43
  (1026 shorter events, 177.9 us)
Async XLA Ops:
  6.5 287.5 %all-gather.3.cloned.1.call-start = ((), (), s32[]{:S(2)}) async-start(), calls=%async_computation | async-start | bytes 1179648 | tf_op jit(solution)/shard_map/all_gather | solution.py:28
  6.5 1.4 copy-start.3
  6.5 1.4 copy-start.5
  295.6 5.4 %copy-start = (f32[128,2048]{1,0:T(8,128)S(1)}, f32[128,2048]{1,0:T(8,128)}, u32[]{:S(2)}) copy-start(f32[128,2048]{1,0:T(8,128)} %get-tuple-element.38) | copy-start | bytes 3145732
  295.7 5.4 %copy-start.1 = (bf16[128,2048]{1,0:T(8,128)(2,1)S(1)}, bf16[128,2048]{1,0:T(8,128)(2,1)}, u32[]{:S(2)}) copy-start(bf16[128,2048]{1,0:T(8,128)(2,1)} %param.11) | copy-start | bytes 1572868
  295.7 5.4 %copy-start.2 = (bf16[128,2048]{1,0:T(8,128)(2,1)S(1)}, bf16[128,2048]{1,0:T(8,128)(2,1)}, u32[]{:S(2)}) copy-start(bf16[128,2048]{1,0:T(8,128)(2,1)} %param.10) | copy-start | bytes 1572868
  295.7 5.4 %copy-start.4 = (bf16[128,2048]{1,0:T(8,128)(2,1)S(1)}, bf16[128,2048]{1,0:T(8,128)(2,1)}, u32[]{:S(2)}) copy-start(bf16[128,2048]{1,0:T(8,128)(2,1)} %param.9) | copy-start | bytes 1572868
  295.7 5.4 %copy-start.6 = (f32[2048]{0:T(1024)S(1)}, f32[2048]{0:T(1024)}, u32[]{:S(2)}) copy-start(f32[2048]{0:T(1024)} %param.14) | copy-start | bytes 24580
  301.1 6.2 %copy-start.7 = (f32[2048]{0:T(1024)S(1)}, f32[2048]{0:T(1024)}, u32[]{:S(2)}) copy-start(f32[2048]{0:T(1024)} %param.15) | copy-start | bytes 24580
Sparse Core Ops, SparseCore 0:
  251.2 42.8 all-gather.2
where the time goes:
time: 319 us; the launch traced here: 315 us
  local copies, waits for them, and re-layouts  145 us (45%)
  other arithmetic  102 us (32%)
  waiting for transfers between devices  43 us (13%)
  between operations  13.6 us (4%)
  loops' own time  5.89 us (2%)
  blocking collectives  5.67 us (2%)
    pad x192, local copies, waits for them, and re-layouts, one_mode(): state = lax.associative_scan(combine_pair, (factors, driven), axis=0)[1]  73 us
    slice x352, local copies, waits for them, and re-layouts, one_mode(): state = lax.associative_scan(combine_pair, (factors, driven), axis=0)[1]  47.6 us
    all_gather x1, waiting for transfers between devices, body(): piece = lax.all_gather(end_states[None], 'ctx', axis=0, tiled=True)  42.9 us
    add x16, other arithmetic, one_mode(): return (total + scale[None, :] * state, state[count - 1])  37.7 us
    dynamic_update_slice x16, local copies, waits for them, and re-layouts, body(): local_part, end_states = lax.scan(one_mode, start, (rates, residues))  23.9 us
    add x192, other arithmetic, combine_pair(): return (first[0] * second[0], first[1] * second[0] + second[1])  22.9 us
    add x112, other arithmetic, one_mode(): state = lax.associative_scan(combine_pair, (factors, driven), axis=0)[1]  15.3 us
    concatenate x96, other arithmetic, one_mode(): state = lax.associative_scan(combine_pair, (factors, driven), axis=0)[1]  15.2 us
  transfers between devices with their start and end apart: 1, of which 1 were waited for; matrix products, arithmetic and copies ran while one was open for 0% of the time, Pallas kernels for 0%

commit v1 on v0

v1 whole, which is shorter than its diff:
```python
import jax
import jax.numpy as jnp
from jax import lax
from jax.experimental import pallas as pl
from jax.experimental.pallas import tpu as pltpu
from jax.sharding import PartitionSpec as P

C = 8192
LANES = 128
ROWS = 8
F32 = jnp.float32


def lanes(group):
    return pl.ds(pl.multiple_of(group * LANES, LANES), LANES)


def own_half_first(x_ref, source, ordered):
    half = source.shape[0] // 2
    first = pl.multiple_of(x_ref[0] * half, half)
    ordered[:half, :] = source[pl.ds(first, half), :]
    ordered[half:, :] = source[pl.ds(pl.multiple_of(half - first, half), half), :]


def end_states_kernel(modes, x_ref, keys, values, rates, mine, other, ordered):
    count, width = keys.shape
    half = modes // 2
    own_half_first(x_ref, rates, ordered)
    below = (ROWS - 1 - lax.broadcasted_iota(jnp.int32, (ROWS, LANES), 0)).astype(F32)

    def group_step(group, unused):
        at = lanes(group)
        driven = keys[:, at].astype(F32) * values[:, at].astype(F32)
        blocks = [driven[i:i + ROWS] for i in range(0, count, ROWS)]
        for start, out in ((0, mine), (half, other)):
            for mode in range(half):
                rate = jnp.broadcast_to(ordered[start + mode:start + mode + 1, at], (ROWS, LANES))
                factor = jnp.exp(-ROWS * rate)
                state = blocks[0]
                for block in blocks[1:]:
                    state = state * factor + block
                state = state * jnp.exp(-rate * below)
                out[mode:mode + 1, at] = jnp.sum(state, axis=0, keepdims=True)
        return unused

    lax.fori_loop(0, width // LANES, group_step, 0)


def local_kernel(modes, query, keys, values, rates, residues, skip, out, series, rate_rows, scale_rows):
    count, width = keys.shape
    groups = width // LANES

    def spread_params(group, unused):
        at = lanes(group)
        for i in range(0, modes, ROWS):
            rows = pl.ds(i * groups + group, ROWS, stride=groups)
            decay = jnp.exp(-rates[i:i + ROWS, at])
            rate_rows[rows, :] = decay
            scale_rows[rows, :] = residues[i:i + ROWS, at] * jnp.sqrt(1.0 - decay * decay)
        return unused

    lax.fori_loop(0, groups, spread_params, 0)

    def spread(group, unused):
        at = lanes(group)
        driven = keys[:, at].astype(F32) * values[:, at].astype(F32)
        for i in range(0, count, ROWS):
            series[pl.ds(i * groups + group, ROWS, stride=groups), :] = driven[i:i + ROWS]
        return unused

    lax.fori_loop(0, groups, spread, 0)

    for part in range(0, groups, ROWS):
        decays = [rate_rows[m * groups + part:m * groups + part + ROWS, :] for m in range(modes)]
        scales = [scale_rows[m * groups + part:m * groups + part + ROWS, :] for m in range(modes)]

        def token(t, states):
            rows = pl.ds(pl.multiple_of(t * groups + part, ROWS), ROWS)
            now = series[rows, :]
            states = [s * d + now for s, d in zip(states, decays)]
            terms = [s * w for s, w in zip(states, scales)]
            while len(terms) > 1:
                terms = [a + b for a, b in zip(terms[::2], terms[1::2])]
            series[rows, :] = terms[0]
            return states

        lax.fori_loop(0, count, token, [jnp.zeros((ROWS, LANES), F32)] * modes, unroll=2)

    def gate(group, unused):
        at = lanes(group)
        driven = keys[:, at].astype(F32) * values[:, at].astype(F32)
        gates = query[:, at].astype(F32)
        through = skip[:, at]
        for i in range(0, count, ROWS):
            filtered = series[pl.ds(i * groups + group, ROWS, stride=groups), :]
            out[i:i + ROWS, at] = gates[i:i + ROWS] * (filtered + through * driven[i:i + ROWS])
        return unused

    lax.fori_loop(0, groups, gate, 0)


def carry_kernel(modes, x_ref, local, query, kept, received, rates, residues, gated, squares, sums, ordered, weights):
    count, width = query.shape
    half = modes // 2
    own_half_first(x_ref, rates, ordered)
    own_half_first(x_ref, residues, weights)
    decay = jnp.exp(-ordered[...])
    weights[...] = weights[...] * jnp.sqrt(1.0 - decay * decay)
    weights[:half, :] *= kept[...]
    weights[half:, :] *= received[...]
    ahead = (1 + lax.broadcasted_iota(jnp.int32, (ROWS, LANES), 0)).astype(F32)
    sums[...] = jnp.zeros_like(sums)

    def group_step(group, unused):
        at = lanes(group)
        gates = query[:, at].astype(F32)
        terms, factors = [], []
        for mode in range(modes):
            rate = jnp.broadcast_to(ordered[mode:mode + 1, at], (ROWS, LANES))
            weight = jnp.broadcast_to(weights[mode:mode + 1, at], (ROWS, LANES))
            terms.append(weight * jnp.exp(-rate * ahead))
            factors.append(jnp.exp(-ROWS * rate))
        for i in range(0, count, ROWS):
            total = terms
            while len(total) > 1:
                total = [a + b for a, b in zip(total[::2], total[1::2])]
            result = local[i:i + ROWS, at] + gates[i:i + ROWS] * total[0]
            gated[i:i + ROWS, at] = result
            sums[i:i + ROWS, :] += result * result
            if i + ROWS < count:
                terms = [t * f for t, f in zip(terms, factors)]
        return unused

    lax.fori_loop(0, width // LANES, group_step, 0)
    squares[...] = jnp.sum(jnp.transpose(sums[...]), axis=0, keepdims=True)


def norm_kernel(gated, gain, *rest):
    *parts, out = rest
    count, width = gated.shape
    total = parts[0][...]
    for part in parts[1:]:
        total = total + part[...]
    factor = lax.rsqrt(total / C + 1e-06)
    factor = jnp.transpose(jnp.broadcast_to(factor, (count, count)))[:, :LANES]

    def group_step(group, unused):
        at = lanes(group)
        out[:, at] = (gated[:, at] * factor * gain[:, at]).astype(out.dtype)
        return unused

    lax.fori_loop(0, width // LANES, group_step, 0)


VMEM = pl.BlockSpec(memory_space=pltpu.VMEM)
SMEM = pl.BlockSpec(memory_space=pltpu.SMEM)


def call(kernel, inputs, outputs, scratch=(), scalar=False, flops=0, name=None):
    size = sum(x.size * x.dtype.itemsize for x in (*inputs, *outputs))
    return pl.pallas_call(
        kernel,
        out_shape=outputs,
        in_specs=[SMEM if scalar and i == 0 else VMEM for i in range(len(inputs))],
        out_specs=[VMEM] * len(outputs),
        scratch_shapes=scratch,
        cost_estimate=pl.CostEstimate(flops=flops, bytes_accessed=size, transcendentals=0),
        compiler_params=pltpu.CompilerParams(vmem_limit_bytes=32 * 1024 * 1024),
        name=name,
    )(*inputs)


def body(ctx, tp, query, keys, values, rates, residues, skip, gain):
    count, width = keys.shape
    modes = rates.shape[0]
    half = modes // 2
    outer = ctx // 2
    f32 = lambda *shape: jax.ShapeDtypeStruct(shape, F32)
    own = lax.axis_index("ctx").astype(jnp.int32)
    z, x = own // 2, own % 2
    x_ref = x.reshape(1)

    mine, other = call(
        lambda *refs: end_states_kernel(modes, *refs),
        (x_ref, keys, values, rates),
        (f32(half, width), f32(half, width)),
        scratch=[pltpu.VMEM((modes, width), F32)],
        scalar=True,
        flops=2 * modes * count * width,
        name="end_states",
    )
    (local,) = call(
        lambda *refs: local_kernel(modes, *refs),
        (query, keys, values, rates, residues, skip[None]),
        (f32(count, width),),
        scratch=[
            pltpu.VMEM((count * width // LANES, LANES), F32),
            pltpu.VMEM((modes * width // LANES, LANES), F32),
            pltpu.VMEM((modes * width // LANES, LANES), F32),
        ],
        flops=4 * modes * count * width,
        name="local_filter",
    )

    pair = [(i, i ^ 1) for i in range(ctx)]

    def shifted(array, by):
        return lax.ppermute(array, "ctx", [(i, (i + 2 * by) % ctx) for i in range(ctx)])

    my_rates = jnp.where(x == 0, rates[:half], rates[half:])
    step = jnp.exp(-my_rates * count)
    partner = lax.ppermute(other, "ctx", pair)
    pair_state = jnp.where(x == 0, mine * step + partner, partner * step + mine)

    span = min(3, outer - 1)
    before = jnp.zeros_like(mine)
    for by, moved in [(by, shifted(pair_state, by)) for by in range(span, 0, -1)]:
        weight = jnp.exp(-my_rates * (2 * count * (by - 1)))
        before = before + jnp.where(z >= by, weight * moved, 0.0)
    while span < outer - 1:
        moves = [(by, shifted(before, by)) for by in range(3 * span, 0, -span) if by < outer]
        for by, moved in moves:
            weight = jnp.exp(-my_rates * (2 * count * by))
            before = before + jnp.where(z >= by, weight * moved, 0.0)
        span = 4 * span

    second = before * step + jnp.where(x == 0, mine, partner)
    kept = jnp.where(x == 0, before, second)
    received = lax.ppermute(jnp.where(x == 0, second, before), "ctx", pair)

    gated, squares = call(
        lambda *refs: carry_kernel(modes, *refs),
        (x_ref, local, query, kept, received, rates, residues),
        (f32(count, width), f32(1, count)),
        scratch=[
            pltpu.VMEM((count, LANES), F32),
            pltpu.VMEM((modes, width), F32),
            pltpu.VMEM((modes, width), F32),
        ],
        scalar=True,
        flops=2 * modes * count * width,
        name="add_carry",
    )
    parts = [squares] + [
        lax.ppermute(squares, "tp", [(i, (i + by) % tp) for i in range(tp)]) for by in range(1, tp)
    ]
    (out,) = call(
        norm_kernel,
        (gated, gain[None], *parts),
        (jax.ShapeDtypeStruct((count, width), jnp.bfloat16),),
        flops=2 * count * width,
        name="norm",
    )
    return out


def solution(mesh):
    ctx, tp = mesh.shape["ctx"], mesh.shape["tp"]
    in_specs = (
        P("ctx", "tp"),
        P("ctx", "tp"),
        P("ctx", "tp"),
        P(None, "tp"),
        P(None, "tp"),
        P("tp"),
        P("tp"),
    )
    return jax.shard_map(
        lambda *arrays: body(ctx, tp, *arrays),
        mesh=mesh,
        in_specs=in_specs,
        out_specs=P("ctx", "tp"),
        check_vma=False,
    )
```

time: 319 us -> 33.7 us (0.11); the launches traced: 315 us -> 33.5 us
  local copies, waits for them, and re-layouts: 145 us -> 3.02 us
  other arithmetic: 102 us -> 0.1 us
  waiting for transfers between devices: 43 us -> 8.16 us
  between operations: 13.6 us -> 0.09 us
  starting transfers between devices: 0.01 us -> 12.5 us
  Pallas kernels: 0 us -> 9.64 us
  loops' own time: 5.89 us -> 0 us
  blocking collectives: 5.67 us -> 0 us
    add x321 -> x0, other arithmetic: 75.9 us -> none  [the longest x16 37.7 us: one_mode(): return (total + scale[None, :] * state, state[count - 1])]
    pad x192 -> x0, local copies, waits for them, and re-layouts: 73 us -> none  [one_mode(): state = lax.associative_scan(combine_pair, (factors, driven), axis=0)[1]]
    slice x352 -> x0, local copies, waits for them, and re-layouts: 47.6 us -> none  [one_mode(): state = lax.associative_scan(combine_pair, (factors, driven), axis=0)[1]]
    all_gather x1 -> x0, waiting for transfers between devices: 42.9 us -> none  [body(): piece = lax.all_gather(end_states[None], 'ctx', axis=0, tiled=True)]
    dynamic_update_slice x16 -> x0, local copies, waits for them, and re-layouts: 23.9 us -> none  [body(): local_part, end_states = lax.scan(one_mode, start, (rates, residues))]
    concatenate x96 -> x0, other arithmetic: 15.2 us -> none  [one_mode(): state = lax.associative_scan(combine_pair, (factors, driven), axis=0)[1]]
    ppermute x0 -> x8, starting transfers between devices: none -> 12.5 us  [the longest x3 6.1 us: shifted(): lax.ppermute(array, 'ctx', [(i, (i + 2 * by) % ctx) for i in range(ctx)])]
    pallas_call x0 -> x4, Pallas kernels: none -> 9.64 us  [call(): pl.pallas_call(kernel, out_shape=outputs, in_specs=[SMEM if scalar and i...]
  transfers between devices with their start and end apart: 1 -> 8, of which waited for: 1 -> 6; matrix products, arithmetic and copies ran while one was open for 0% -> 0% of each run, Pallas kernels for 0% -> 14%
where the time goes in v1:
time: 33.7 us; the launch traced here: 33.5 us
  starting transfers between devices  12.5 us (37%)
  Pallas kernels  9.64 us (29%)
  waiting for transfers between devices  8.16 us (24%)
  local copies, waits for them, and re-layouts  3.02 us (9%)
    pallas_call x4, Pallas kernels, call(): pl.pallas_call(kernel, out_shape=outputs, in_specs=[SMEM if scalar and i...  9.64 us
    ppermute x3, starting transfers between devices, shifted(): lax.ppermute(array, 'ctx', [(i, (i + 2 * by) % ctx) for i in range(ctx)])  6.1 us
    ppermute x3, waiting for transfers between devices, shifted(): lax.ppermute(array, 'ctx', [(i, (i + 2 * by) % ctx) for i in range(ctx)])  3.11 us
    unnamed x20, local copies, waits for them, and re-layouts  3.02 us
    ppermute x1, starting transfers between devices, body(): partner = lax.ppermute(other, 'ctx', pair)  3 us
    ppermute x3, waiting for transfers between devices, body(): lax.ppermute(squares, 'tp', [(i, (i + by) % tp) for i in range(tp)])  2.8 us
    ppermute x1, waiting for transfers between devices, body(): partner = lax.ppermute(other, 'ctx', pair)  2.25 us
    ppermute x3, starting transfers between devices, body(): lax.ppermute(squares, 'tp', [(i, (i + by) % tp) for i in range(tp)])  1.81 us
  transfers between devices with their start and end apart: 8, of which 6 were waited for; matrix products, arithmetic and copies ran while one was open for 0% of the time, Pallas kernels for 14%

profile of v1, /device:TPU:0, one launch (start us, length us, event | category | flops | bytes accessed | tf_op | source)
XLA Modules:
  0.0 33.5 jit_solution(15231602986630101785)
XLA Ops:
  0.0 0.9 %copy-done = f32[16,2048]{1,0:T(8,128)S(1)} copy-done((f32[16,2048]{1,0:T(8,128)S(1)}, f32[16,2048]{1,0:T(8,128)}, u32[]{:S(2)}) %copy-start) | copy-done | bytes 131096
  0.9 1.0 %copy-done.3 = bf16[128,2048]{1,0:T(8,128)(2,1)S(1)} copy-done((bf16[128,2048]{1,0:T(8,128)(2,1)S(1)}, bf16[128,2048]{1,0:T(8,128)(2,1)}, u32[]{:S(2)}) %copy-start.3) | copy-done | bytes 524312
  1.9 1.0 %copy-done.5 = bf16[128,2048]{1,0:T(8,128)(2,1)S(1)} copy-done((bf16[128,2048]{1,0:T(8,128)(2,1)S(1)}, bf16[128,2048]{1,0:T(8,128)(2,1)}, u32[]{:S(2)}) %copy-start.5) | copy-done | bytes 524312
  3.0 2.0 %end_states.1 = (f32[8,2048]{1,0:T(8,128)S(1)}, f32[8,2048]{1,0:T(8,128)S(1)}) custom-call(s32[1]{0:T(128)} %bitcast.refs_0_, bf16[128,2048]{1,0:T(8,128)(2,1)S(1)} %copy-done.3, bf16[128,2048]{1,0:T(8,128)(2,1)S(1)} %copy-done.5, f32[16,2048]{1,0:T(8,128)S(1)} %copy-done), custom_call_target="tpu_custom_call" | custom-call | flops 8388608 | bytes 1310724 | tf_op jit(solution)/shard_map/end_states/pallas_call | solution.py:161
  5.0 0.0 copy-start.2
  5.0 3.0 %collective-permute-start = (f32[8,2048]{1,0:T(8,128)S(1)}, f32[8,2048]{1,0:T(8,128)S(1)}, u32[]{:S(2)}, u32[]{:S(2)}) collective-permute-start(f32[8,2048]{1,0:T(8,128)S(1)} %get-tuple-element.10), channel_id=1, source_target_pairs={{0,4},{4,0},{8,12},{12,8},{16,20},{20,16},{24,28},{28,24},{1,5},{5... | collective-permute-start | bytes 196616 | tf_op jit(solution)/shard_map/ppermute | solution.py:212
  8.0 2.2 %collective-permute-done = f32[8,2048]{1,0:T(8,128)S(1)} collective-permute-done((f32[8,2048]{1,0:T(8,128)S(1)}, f32[8,2048]{1,0:T(8,128)S(1)}, u32[]{:S(2)}, u32[]{:S(2)}) %collective-permute-start) | collective-permute-done | bytes 65568 | tf_op jit(solution)/shard_map/ppermute | solution.py:212
  10.2 0.0 copy-done.1
  10.3 2.2 %collective-permute-start.3 = (f32[8,2048]{1,0:T(8,128)S(1)}, f32[8,2048]{1,0:T(8,128)S(1)}, u32[]{:S(2)}, u32[]{:S(2)}) collective-permute-start(f32[8,2048]{1,0:T(8,128)S(1)} %add_select_fusion), channel_id=1, source_target_pairs={{0,8},{4,12},{8,16},{12,20},{16,24},{20,28},{24,0},{28,4},{1,9},{5... | collective-permute-start | bytes 196616 | tf_op jit(solution)/shard_map/ppermute | solution.py:208
  12.4 2.6 %collective-permute-start.2 = (f32[8,2048]{1,0:T(8,128)S(1)}, f32[8,2048]{1,0:T(8,128)S(1)}, u32[]{:S(2)}, u32[]{:S(2)}) collective-permute-start(f32[8,2048]{1,0:T(8,128)S(1)} %add_select_fusion), channel_id=1, source_target_pairs={{0,16},{4,20},{8,24},{12,28},{16,0},{20,4},{24,8},{28,12},{1,17},{... | collective-permute-start | bytes 196616 | tf_op jit(solution)/shard_map/ppermute | solution.py:208
  15.0 1.3 %collective-permute-start.1 = (f32[8,2048]{1,0:T(8,128)S(1)}, f32[8,2048]{1,0:T(8,128)S(1)}, u32[]{:S(2)}, u32[]{:S(2)}) collective-permute-start(f32[8,2048]{1,0:T(8,128)S(1)} %add_select_fusion), channel_id=1, source_target_pairs={{0,24},{4,28},{8,0},{12,4},{16,8},{20,12},{24,16},{28,20},{1,25},{... | collective-permute-start | bytes 196616 | tf_op jit(solution)/shard_map/ppermute | solution.py:208
  16.4 1.0 %collective-permute-done.3 = f32[8,2048]{1,0:T(8,128)S(1)} collective-permute-done((f32[8,2048]{1,0:T(8,128)S(1)}, f32[8,2048]{1,0:T(8,128)S(1)}, u32[]{:S(2)}, u32[]{:S(2)}) %collective-permute-start.3) | collective-permute-done | bytes 65568 | tf_op jit(solution)/shard_map/ppermute | solution.py:208
  17.3 1.7 %collective-permute-done.2 = f32[8,2048]{1,0:T(8,128)S(1)} collective-permute-done((f32[8,2048]{1,0:T(8,128)S(1)}, f32[8,2048]{1,0:T(8,128)S(1)}, u32[]{:S(2)}, u32[]{:S(2)}) %collective-permute-start.2) | collective-permute-done | bytes 65568 | tf_op jit(solution)/shard_map/ppermute | solution.py:208
  19.0 0.5 %collective-permute-done.1 = f32[8,2048]{1,0:T(8,128)S(1)} collective-permute-done((f32[8,2048]{1,0:T(8,128)S(1)}, f32[8,2048]{1,0:T(8,128)S(1)}, u32[]{:S(2)}, u32[]{:S(2)}) %collective-permute-start.1) | collective-permute-done | bytes 65568 | tf_op jit(solution)/shard_map/ppermute | solution.py:208
  19.5 0.1 broadcast_select_fusion
  19.5 1.6 %collective-permute-start.4 = (f32[8,2048]{1,0:T(8,128)S(1)}, f32[8,2048]{1,0:T(8,128)S(1)}, u32[]{:S(2)}, u32[]{:S(2)}) collective-permute-start(f32[8,2048]{1,0:T(8,128)S(1)} %get-tuple-element.13), channel_id=1, source_target_pairs={{0,4},{4,0},{8,12},{12,8},{16,20},{20,16},{24,28},{28,24},{1,5},{5... | collective-permute-start | bytes 196616 | tf_op jit(solution)/shard_map/ppermute | solution.py:229
  21.1 0.0 copy-done.4
  21.1 0.0 copy-done.6
  21.1 0.0 copy-done.2
  21.1 0.0 copy-done.7
  21.1 0.0 copy-done.8
  21.1 4.8 %local_filter.1.refs_1_ = f32[128,2048]{1,0:T(8,128)S(1)} custom-call(bf16[128,2048]{1,0:T(8,128)(2,1)S(1)} %copy-done.2, bf16[128,2048]{1,0:T(8,128)(2,1)S(1)} %copy-done.4, bf16[128,2048]{1,0:T(8,128)(2,1)S(1)} %copy-done.6, f32[16,2048]{1,0:T(8,128)S(1)} %copy-done.1, f32[16,2048]{1,0:T(8,128)S(1)} %copy-done.7, f32[1,2048]{1,0:T(1,128)S(1)} %bitcast.3), custom_call_target="tpu_custom_call" | custom-call | flops 16777216 | bytes 2891776 | tf_op jit(solution)/shard_map/local_filter/pallas_call | solution.py:161
  25.9 0.0 collective-permute-done.4.refs_4_
  25.9 0.0 copy-start.9
  25.9 1.8 %add_carry.1 = (f32[128,2048]{1,0:T(8,128)S(1)}, f32[1,128]{1,0:T(1,128)S(1)}) custom-call(s32[1]{0:T(128)} %bitcast.refs_0_, f32[128,2048]{1,0:T(8,128)S(1)} %local_filter.1.refs_1_, bf16[128,2048]{1,0:T(8,128)(2,1)S(1)} %copy-done.2, f32[8,2048]{1,0:T(8,128)S(1)} %get-tuple-element.14.refs_3_, f32[8,2048]{1,0:T(8,128)S(1)} %collective-permute-done.4.refs_4_, ...), custom_call_target="tpu_custom_call" | custom-call | flops 8388608 | bytes 3015172 | tf_op jit(solution)/shard_map/add_carry/pallas_call | solution.py:161
  27.7 0.1 collective-permute-start.7
  27.8 1.6 %collective-permute-start.6 = (f32[1,128]{1,0:T(1,128)S(1)}, f32[1,128]{1,0:T(1,128)S(1)}, u32[]{:S(2)}, u32[]{:S(2)}) collective-permute-start(f32[1,128]{1,0:T(1,128)S(1)} %get-tuple-element.12.rest_0_), channel_id=1, source_target_pairs={{0,2},{1,3},{2,0},{3,1},{4,6},{5,7},{6,4},{7,5},{8,10},{9,11},{10,... | collective-permute-start | bytes 1544 | tf_op jit(solution)/shard_map/ppermute | solution.py:245
  29.4 0.2 collective-permute-start.5
  29.5 0.0 collective-permute-done.7.rest_3_
  29.5 1.9 %collective-permute-done.6.rest_2_ = f32[1,128]{1,0:T(1,128)S(1)} collective-permute-done((f32[1,128]{1,0:T(1,128)S(1)}, f32[1,128]{1,0:T(1,128)S(1)}, u32[]{:S(2)}, u32[]{:S(2)}) %collective-permute-start.6) | collective-permute-done | bytes 544 | tf_op jit(solution)/shard_map/ppermute | solution.py:245
  31.4 0.9 %collective-permute-done.5.rest_1_ = f32[1,128]{1,0:T(1,128)S(1)} collective-permute-done((f32[1,128]{1,0:T(1,128)S(1)}, f32[1,128]{1,0:T(1,128)S(1)}, u32[]{:S(2)}, u32[]{:S(2)}) %collective-permute-start.5) | collective-permute-done | bytes 544 | tf_op jit(solution)/shard_map/ppermute | solution.py:245
  32.3 1.1 %norm.1 = bf16[128,2048]{1,0:T(8,128)(2,1)} custom-call(f32[128,2048]{1,0:T(8,128)S(1)} %get-tuple-element.11.gated, f32[1,2048]{1,0:T(1,128)S(1)} %bitcast.4, f32[1,128]{1,0:T(1,128)S(1)} %get-tuple-element.12.rest_0_, f32[1,128]{1,0:T(1,128)S(1)} %collective-permute-done.5.rest_1_, f32[1,128]{1,0:T(1,128)S(1)} %collective-permute-done.6.rest_2_, ...), custom_call_target="tpu_custom_call" | custom-call | flops 524288 | bytes 1583104 | tf_op jit(solution)/shard_map/norm/pallas_call | solution.py:161
  (10 shorter events, 0.0 us)
Async XLA Ops:
  0.0 0.9 %copy-start = (f32[16,2048]{1,0:T(8,128)S(1)}, f32[16,2048]{1,0:T(8,128)}, u32[]{:S(2)}) copy-start(f32[16,2048]{1,0:T(8,128)} %refs_5_.1) | copy-start | bytes 393220
  0.9 1.0 %copy-start.3 = (bf16[128,2048]{1,0:T(8,128)(2,1)S(1)}, bf16[128,2048]{1,0:T(8,128)(2,1)}, u32[]{:S(2)}) copy-start(bf16[128,2048]{1,0:T(8,128)(2,1)} %refs_1_.3) | copy-start | bytes 1572868
  1.9 1.0 %copy-start.5 = (bf16[128,2048]{1,0:T(8,128)(2,1)S(1)}, bf16[128,2048]{1,0:T(8,128)(2,1)}, u32[]{:S(2)}) copy-start(bf16[128,2048]{1,0:T(8,128)(2,1)} %refs_2_.4) | copy-start | bytes 1572868
  3.0 7.2 %copy-start.1 = (f32[16,2048]{1,0:T(8,128)S(1)}, f32[16,2048]{1,0:T(8,128)}, u32[]{:S(2)}) copy-start(f32[16,2048]{1,0:T(8,128)} %refs_5_.1) | copy-start | bytes 393220
  3.0 18.1 %copy-start.4 = (bf16[128,2048]{1,0:T(8,128)(2,1)S(1)}, bf16[128,2048]{1,0:T(8,128)(2,1)}, u32[]{:S(2)}) copy-start(bf16[128,2048]{1,0:T(8,128)(2,1)} %refs_1_.3) | copy-start | bytes 1572868
  3.0 18.1 %copy-start.6 = (bf16[128,2048]{1,0:T(8,128)(2,1)S(1)}, bf16[128,2048]{1,0:T(8,128)(2,1)}, u32[]{:S(2)}) copy-start(bf16[128,2048]{1,0:T(8,128)(2,1)} %refs_2_.4) | copy-start | bytes 1572868
  5.0 16.1 %copy-start.2 = (bf16[128,2048]{1,0:T(8,128)(2,1)S(1)}, bf16[128,2048]{1,0:T(8,128)(2,1)}, u32[]{:S(2)}) copy-start(bf16[128,2048]{1,0:T(8,128)(2,1)} %refs_2_.5) | copy-start | bytes 1572868
  5.0 5.2 %collective-permute-start = (f32[8,2048]{1,0:T(8,128)S(1)}, f32[8,2048]{1,0:T(8,128)S(1)}, u32[]{:S(2)}, u32[]{:S(2)}) collective-permute-start(f32[8,2048]{1,0:T(8,128)S(1)} %get-tuple-element.10), channel_id=1, source_target_pairs={{0,4},{4,0},{8,12},{12,8},{16,20},{20,16},{24,28},{28,24},{1,5},{5... | collective-permute-start | bytes 196616 | tf_op jit(solution)/shard_map/ppermute | solution.py:212
  10.3 7.1 %collective-permute-start.3 = (f32[8,2048]{1,0:T(8,128)S(1)}, f32[8,2048]{1,0:T(8,128)S(1)}, u32[]{:S(2)}, u32[]{:S(2)}) collective-permute-start(f32[8,2048]{1,0:T(8,128)S(1)} %add_select_fusion), channel_id=1, source_target_pairs={{0,8},{4,12},{8,16},{12,20},{16,24},{20,28},{24,0},{28,4},{1,9},{5... | collective-permute-start | bytes 196616 | tf_op jit(solution)/shard_map/ppermute | solution.py:208
  12.4 6.6 %collective-permute-start.2 = (f32[8,2048]{1,0:T(8,128)S(1)}, f32[8,2048]{1,0:T(8,128)S(1)}, u32[]{:S(2)}, u32[]{:S(2)}) collective-permute-start(f32[8,2048]{1,0:T(8,128)S(1)} %add_select_fusion), channel_id=1, source_target_pairs={{0,16},{4,20},{8,24},{12,28},{16,0},{20,4},{24,8},{28,12},{1,17},{... | collective-permute-start | bytes 196616 | tf_op jit(solution)/shard_map/ppermute | solution.py:208
  15.0 4.5 %collective-permute-start.1 = (f32[8,2048]{1,0:T(8,128)S(1)}, f32[8,2048]{1,0:T(8,128)S(1)}, u32[]{:S(2)}, u32[]{:S(2)}) collective-permute-start(f32[8,2048]{1,0:T(8,128)S(1)} %add_select_fusion), channel_id=1, source_target_pairs={{0,24},{4,28},{8,0},{12,4},{16,8},{20,12},{24,16},{28,20},{1,25},{... | collective-permute-start | bytes 196616 | tf_op jit(solution)/shard_map/ppermute | solution.py:208
  16.4 4.8 %copy-start.7 = (f32[16,2048]{1,0:T(8,128)S(1)}, f32[16,2048]{1,0:T(8,128)}, u32[]{:S(2)}) copy-start(f32[16,2048]{1,0:T(8,128)} %refs_6_.1) | copy-start | bytes 393220
  19.5 1.6 %copy-start.8 = (f32[2048]{0:T(1024)S(1)}, f32[2048]{0:T(1024)}, u32[]{:S(2)}) copy-start(f32[2048]{0:T(1024)} %param.12) | copy-start | bytes 24580
  19.5 6.4 %collective-permute-start.4 = (f32[8,2048]{1,0:T(8,128)S(1)}, f32[8,2048]{1,0:T(8,128)S(1)}, u32[]{:S(2)}, u32[]{:S(2)}) collective-permute-start(f32[8,2048]{1,0:T(8,128)S(1)} %get-tuple-element.13), channel_id=1, source_target_pairs={{0,4},{4,0},{8,12},{12,8},{16,20},{20,16},{24,28},{28,24},{1,5},{5... | collective-permute-start | bytes 196616 | tf_op jit(solution)/shard_map/ppermute | solution.py:229
  25.9 6.4 %copy-start.9 = (f32[2048]{0:T(1024)S(1)}, f32[2048]{0:T(1024)}, u32[]{:S(2)}) copy-start(f32[2048]{0:T(1024)} %param.13) | copy-start | bytes 24580
  27.7 1.8 %collective-permute-start.7 = (f32[1,128]{1,0:T(1,128)S(1)}, f32[1,128]{1,0:T(1,128)S(1)}, u32[]{:S(2)}, u32[]{:S(2)}) collective-permute-start(f32[1,128]{1,0:T(1,128)S(1)} %get-tuple-element.12.rest_0_), channel_id=1, source_target_pairs={{0,3},{1,0},{2,1},{3,2},{4,7},{5,4},{6,5},{7,6},{8,11},{9,8},{10,9... | collective-permute-start | bytes 1544 | tf_op jit(solution)/shard_map/ppermute | solution.py:245
  27.8 3.6 %collective-permute-start.6 = (f32[1,128]{1,0:T(1,128)S(1)}, f32[1,128]{1,0:T(1,128)S(1)}, u32[]{:S(2)}, u32[]{:S(2)}) collective-permute-start(f32[1,128]{1,0:T(1,128)S(1)} %get-tuple-element.12.rest_0_), channel_id=1, source_target_pairs={{0,2},{1,3},{2,0},{3,1},{4,6},{5,7},{6,4},{7,5},{8,10},{9,11},{10,... | collective-permute-start | bytes 1544 | tf_op jit(solution)/shard_map/ppermute | solution.py:245
  29.4 3.0 %collective-permute-start.5 = (f32[1,128]{1,0:T(1,128)S(1)}, f32[1,128]{1,0:T(1,128)S(1)}, u32[]{:S(2)}, u32[]{:S(2)}) collective-permute-start(f32[1,128]{1,0:T(1,128)S(1)} %get-tuple-element.12.rest_0_), channel_id=1, source_target_pairs={{0,1},{1,2},{2,3},{3,0},{4,5},{5,6},{6,7},{7,4},{8,9},{9,10},{10,1... | collective-permute-start | bytes 1544 | tf_op jit(solution)/shard_map/ppermute | solution.py:245

commit v2 on v0

v2 whole, which is shorter than its diff:
```python
import jax
import jax.numpy as jnp
from jax import lax
from jax.experimental import pallas as pl
from jax.experimental.pallas import tpu as pltpu
from jax.sharding import PartitionSpec as P

C = 8192
LANES = 128
ROWS = 8
F32 = jnp.float32
VMEM = pl.BlockSpec(memory_space=pltpu.VMEM)
SMEM = pl.BlockSpec(memory_space=pltpu.SMEM)
HBM = pl.BlockSpec(memory_space=pltpu.HBM)


def lanes(group):
    return pl.ds(pl.multiple_of(group * LANES, LANES), LANES)


def added(terms):
    terms = list(terms)
    while len(terms) > 1:
        terms = [a + b for a, b in zip(terms[::2], terms[1::2])]
    return terms[0]


def spread_row(ref, row, at):
    return jnp.broadcast_to(ref[row:row + 1, at], (ROWS, LANES))


def end_states(blocks, decay, decay8, decay16, turn, out, at):
    modes = decay.shape[0]
    for mode in range(modes):
        factor = spread_row(decay16, mode, at)
        even, odd = blocks[0], blocks[1]
        for i in range(2, len(blocks), 2):
            even = even * factor + blocks[i]
            odd = odd * factor + blocks[i + 1]
        turn[mode * ROWS:(mode + 1) * ROWS, :] = even * spread_row(decay8, mode, at) + odd
    step = decay[:, at]
    state = turn[pl.ds(0, modes, stride=ROWS), :]
    for token in range(1, ROWS):
        state = state * step + turn[pl.ds(token, modes, stride=ROWS), :]
    out[:, at] = state


def set_decays(rate, decay, decay8, decay16):
    decay[...] = jnp.exp(-rate)
    decay8[...] = jnp.exp(-ROWS * rate)
    decay16[...] = jnp.exp(-2 * ROWS * rate)


def first_ends_kernel(chunks, x_ref, keys, values, rates, other, driven, key_buf, value_buf, rate_buf,
                      decay, decay8, decay16, turn, sems):
    count, width = key_buf.shape
    half = rate_buf.shape[0]
    size = width // chunks
    start = pl.multiple_of((1 - x_ref[0]) * half, half)
    rate_copy = pltpu.make_async_copy(rates.at[pl.ds(start, half), :], rate_buf, sems.at[2 * chunks])
    rate_copy.start()
    copies = []
    for i in range(chunks):
        at = pl.ds(i * size, size)
        for j, (source, target) in enumerate(((keys, key_buf), (values, value_buf))):
            copies.append(pltpu.make_async_copy(source.at[:, at], target.at[:, at], sems.at[2 * i + j]))
            copies[-1].start()
    rate_copy.wait()
    set_decays(rate_buf[...], decay, decay8, decay16)

    def group_step(group, unused):
        at = lanes(group)
        product = key_buf[:, at].astype(F32) * value_buf[:, at].astype(F32)
        driven[:, at] = product
        blocks = [product[i:i + ROWS] for i in range(0, count, ROWS)]
        end_states(blocks, decay, decay8, decay16, turn.at[group % 2], other, at)
        return unused

    groups = size // LANES
    for i in range(chunks):
        copies[2 * i].wait()
        copies[2 * i + 1].wait()
        lax.fori_loop(i * groups, (i + 1) * groups, group_step, 0, unroll=min(2, groups))


def second_ends_kernel(x_ref, driven, rates, mine, decay, decay8, decay16, turn):
    count, width = driven.shape
    half = rates.shape[0] // 2
    set_decays(rates[pl.ds(pl.multiple_of(x_ref[0] * half, half), half), :], decay, decay8, decay16)

    def group_step(group, unused):
        at = lanes(group)
        blocks = [driven[i:i + ROWS, at] for i in range(0, count, ROWS)]
        end_states(blocks, decay, decay8, decay16, turn.at[group % 2], mine, at)
        return unused

    lax.fori_loop(0, width // LANES, group_step, 0, unroll=2)


def local_kernel(part, query, driven, rates, residues, skip, out, series, decays, scales):
    count = driven.shape[0]
    modes = rates.shape[0]

    def spread(i, unused):
        here = lanes(i)
        at = lanes(part * ROWS + i)
        for mode in range(0, modes, ROWS):
            rows = pl.ds(mode * ROWS + i, ROWS, stride=ROWS)
            decay = jnp.exp(-rates[mode:mode + ROWS, at])
            decays[rows, :] = decay
            scales[rows, :] = residues[mode:mode + ROWS, at] * jnp.sqrt(1.0 - decay * decay)
        for token in range(0, count, ROWS):
            series[pl.ds(token * ROWS + i, ROWS, stride=ROWS), :] = driven[token:token + ROWS, at]
        return unused

    lax.fori_loop(0, ROWS, spread, 0, unroll=2)
    decay = [decays[m * ROWS:(m + 1) * ROWS, :] for m in range(modes)]
    scale = [scales[m * ROWS:(m + 1) * ROWS, :] for m in range(modes)]

    def token_step(token, states):
        rows = pl.ds(pl.multiple_of(token * ROWS, ROWS), ROWS)
        now = series[rows, :]
        states = [s * d + now for s, d in zip(states, decay)]
        series[rows, :] = added(s * w for s, w in zip(states, scale))
        return states

    lax.fori_loop(0, count, token_step, [jnp.zeros((ROWS, LANES), F32)] * modes, unroll=8)

    def gate(i, unused):
        here = lanes(i)
        at = lanes(part * ROWS + i)
        gates = query[:, at].astype(F32)
        for token in range(0, count, ROWS):
            filtered = series[pl.ds(token * ROWS + i, ROWS, stride=ROWS), :]
            out[token:token + ROWS, here] = gates[token:token + ROWS] * (
                filtered + skip[:, at] * driven[token:token + ROWS, at]
            )
        return unused

    lax.fori_loop(0, ROWS, gate, 0, unroll=2)


def carry_kernel(which, pieces, final, x_ref, *refs):
    locals_, (query, carried, rates, residues), rest = refs[:pieces], refs[pieces:pieces + 4], refs[pieces + 4:]
    if final:
        gated, squares, decay, decay8, weights, turn, sums = rest
        sums[...] = jnp.zeros_like(sums)
    else:
        gated, decay, decay8, weights, turn = rest
    count, width = query.shape
    half = carried.shape[0]
    mine = x_ref[0] if which == 0 else 1 - x_ref[0]
    rows = pl.ds(pl.multiple_of(mine * half, half), half)
    rate = rates[rows, :]
    step = jnp.exp(-rate)
    decay[...] = step
    decay8[...] = jnp.exp(-ROWS * rate)
    weights[...] = residues[rows, :] * jnp.sqrt(1.0 - step * step) * carried[...]
    groups = width // LANES // pieces

    for piece, local in enumerate(locals_):
        def group_step(group, unused):
            here = lanes(group)
            at = lanes(piece * groups + group)
            slot = turn.at[group % 2]
            gates = query[:, at].astype(F32)
            term, factor = weights[:, at], decay[:, at]
            for token in range(ROWS):
                term = term * factor
                slot[pl.ds(token, half, stride=ROWS), :] = term
            terms = [slot[m * ROWS:(m + 1) * ROWS, :] for m in range(half)]
            factors = [spread_row(decay8, m, at) for m in range(half)]
            for i in range(0, count, ROWS):
                result = local[i:i + ROWS, here] + gates[i:i + ROWS] * added(terms)
                gated[i:i + ROWS, at] = result
                if final:
                    sums[i:i + ROWS, :] += result * result
                if i + ROWS < count:
                    terms = [t * f for t, f in zip(terms, factors)]
            return unused

        lax.fori_loop(0, groups, group_step, 0)
    if final:
        squares[...] = jnp.sum(jnp.transpose(sums[...]), axis=0, keepdims=True)


def norm_kernel(parts, gated, gain, *rest):
    sums, (out, factors, buf, sems) = rest[:parts], rest[parts:]
    count, width = gated.shape
    factor = lax.rsqrt(added(part[...] for part in sums) / C + 1e-06)
    factors[...] = jnp.transpose(jnp.broadcast_to(factor, (LANES, count)))
    size = 2 * ROWS

    def copy(i):
        rows = pl.ds(pl.multiple_of(i * size, size), size)
        return pltpu.make_async_copy(buf.at[rows, :], out.at[rows, :], sems.at[i])

    def chunk_step(i, unused):
        rows = pl.ds(pl.multiple_of(i * size, size), size)
        factor = factors[rows, :]
        for group in range(width // LANES):
            at = slice(group * LANES, (group + 1) * LANES)
            buf[rows, at] = (gated[rows, at] * factor * gain[:, at]).astype(buf.dtype)
        copy(i).start()
        return unused

    lax.fori_loop(0, count // size, chunk_step, 0)
    for i in range(count // size):
        copy(i).wait()


def call(kernel, inputs, specs, outputs, out_specs=None, scratch=(), flops=0, name=None):
    size = sum(x.size * x.dtype.itemsize for x in (*inputs, *outputs))
    return pl.pallas_call(
        kernel,
        out_shape=outputs,
        in_specs=specs,
        out_specs=out_specs or [VMEM] * len(outputs),
        scratch_shapes=scratch,
        cost_estimate=pl.CostEstimate(flops=flops, bytes_accessed=size, transcendentals=0),
        compiler_params=pltpu.CompilerParams(vmem_limit_bytes=32 * 1024 * 1024),
        name=name,
    )(*inputs)


def body(ctx, tp, query, keys, values, rates, residues, skip, gain):
    count, width = keys.shape
    modes = rates.shape[0]
    half = modes // 2
    outer = ctx // 2
    f32 = lambda *shape: jax.ShapeDtypeStruct(shape, F32)
    vmem = lambda *shape: pltpu.VMEM(shape, F32)
    in_hbm = lambda x: pltpu.with_memory_space_constraint(x, pltpu.HBM)
    tied = lax.optimization_barrier
    own = lax.axis_index("ctx").astype(jnp.int32)
    z, x = own // 2, own % 2
    x_ref = x.reshape(1)
    work = 2 * half * count * width
    pair = [(i, i ^ 1) for i in range(ctx)]

    chunks = width // 256
    other, driven = call(
        lambda *refs: first_ends_kernel(chunks, *refs),
        (x_ref, in_hbm(keys), in_hbm(values), in_hbm(rates)),
        [SMEM, HBM, HBM, HBM],
        (f32(half, width), f32(count, width)),
        scratch=[
            pltpu.VMEM((count, width), keys.dtype),
            pltpu.VMEM((count, width), values.dtype),
            *[vmem(half, width)] * 4,
            vmem(2, half * ROWS, LANES),
            pltpu.SemaphoreType.DMA((2 * chunks + 1,)),
        ],
        flops=work,
        name="first_ends",
    )
    partner = lax.ppermute(other, "ctx", pair)
    (mine,) = call(
        second_ends_kernel,
        (x_ref, driven, rates),
        [SMEM, VMEM, VMEM],
        (f32(half, width),),
        scratch=[*[vmem(half, width)] * 3, vmem(2, half * ROWS, LANES)],
        flops=work,
        name="second_ends",
    )

    pieces = width // LANES // ROWS

    def local_part(part, driven):
        (local,) = call(
            lambda *refs: local_kernel(part, *refs),
            (query, driven, rates, residues, skip[None]),
            [VMEM] * 5,
            (f32(count, width // pieces),),
            scratch=[vmem(count * ROWS, LANES), vmem(modes * ROWS, LANES), vmem(modes * ROWS, LANES)],
            flops=4 * work // pieces,
            name="local_filter",
        )
        return local

    early = [local_part(part, driven) for part in range(pieces // 2)]
    partner, mine, early = tied((partner, mine, early))

    def shifted(array, by):
        return lax.ppermute(array, "ctx", [(i, (i + 2 * by) % ctx) for i in range(ctx)])

    my_rates = jnp.where(x == 0, rates[:half], rates[half:])
    step = jnp.exp(-my_rates * count)
    pair_state = jnp.where(x == 0, mine * step + partner, partner * step + mine)
    pair_state, driven = tied((pair_state, driven))

    span = min(3, outer - 1)
    moved = [shifted(pair_state, by) for by in range(span, 0, -1)]
    late = [local_part(part, driven) for part in range(pieces // 2, pieces)]
    moved, late = tied((moved, late))
    before = jnp.zeros_like(mine)
    for by, states in zip(range(span, 0, -1), moved):
        weight = jnp.exp(-my_rates * (2 * count * (by - 1)))
        before = before + jnp.where(z >= by, weight * states, 0.0)
    while span < outer - 1:
        moved = [(by, shifted(before, by)) for by in range(3 * span, 0, -span) if by < outer]
        for by, states in moved:
            weight = jnp.exp(-my_rates * (2 * count * by))
            before = before + jnp.where(z >= by, weight * states, 0.0)
        span = 4 * span

    second = before * step + jnp.where(x == 0, mine, partner)
    kept = jnp.where(x == 0, before, second)
    received = lax.ppermute(jnp.where(x == 0, second, before), "ctx", pair)

    carry_scratch = [*[vmem(half, width)] * 3, vmem(2, half * ROWS, LANES)]
    locals_ = early + late
    (halfway,) = call(
        lambda *refs: carry_kernel(0, pieces, False, *refs),
        (x_ref, *locals_, query, kept, rates, residues),
        [SMEM] + [VMEM] * (pieces + 4),
        (f32(count, width),),
        scratch=carry_scratch,
        flops=work,
        name="add_kept",
    )
    gated, squares = call(
        lambda *refs: carry_kernel(1, 1, True, *refs),
        (x_ref, halfway, query, received, rates, residues),
        [SMEM] + [VMEM] * 5,
        (f32(count, width), f32(1, count)),
        scratch=[*carry_scratch, vmem(count, LANES)],
        flops=work,
        name="add_received",
    )

    parts = [squares]
    if tp & (tp - 1) == 0:
        mask = 1
        while mask < tp:
            parts = [added(parts)]
            parts.append(lax.ppermute(parts[0], "tp", [(i, i ^ mask) for i in range(tp)]))
            mask = 2 * mask + 1
    else:
        total = squares
        for by in range(1, tp):
            total = total + lax.ppermute(squares, "tp", [(i, (i + by) % tp) for i in range(tp)])
        parts = [total]
    (out,) = call(
        lambda *refs: norm_kernel(len(parts), *refs),
        (gated, gain[None], *parts),
        [VMEM] * (2 + len(parts)),
        (jax.ShapeDtypeStruct((count, width), query.dtype),),
        out_specs=[HBM],
        scratch=[
            vmem(count, LANES),
            pltpu.VMEM((count, width), query.dtype),
            pltpu.SemaphoreType.DMA((count // (2 * ROWS),)),
        ],
        flops=2 * count * width,
        name="norm",
    )
    return out


def solution(mesh):
    ctx, tp = mesh.shape["ctx"], mesh.shape["tp"]
    in_specs = (
        P("ctx", "tp"),
        P("ctx", "tp"),
        P("ctx", "tp"),
        P(None, "tp"),
        P(None, "tp"),
        P("tp"),
        P("tp"),
    )
    return jax.shard_map(
        lambda *arrays: body(ctx, tp, *arrays),
        mesh=mesh,
        in_specs=in_specs,
        out_specs=P("ctx", "tp"),
        check_vma=False,
    )
```

time: 319 us -> 27.7 us (0.09); the launches traced: 315 us -> 27.5 us
  local copies, waits for them, and re-layouts: 145 us -> 0.24 us
  other arithmetic: 102 us -> 0.11 us
  waiting for transfers between devices: 43 us -> 6.49 us
  between operations: 13.6 us -> 0.08 us
  starting transfers between devices: 0.01 us -> 11.4 us
  Pallas kernels: 0 us -> 9.21 us
  loops' own time: 5.89 us -> 0 us
  blocking collectives: 5.67 us -> 0 us
    add x321 -> x1, other arithmetic: 75.9 us -> 0.01 us  [added(): terms = [a + b for a, b in zip(terms[::2], terms[1::2])]]
    pad x192 -> x0, local copies, waits for them, and re-layouts: 73 us -> none  [one_mode(): state = lax.associative_scan(combine_pair, (factors, driven), axis=0)[1]]
    slice x352 -> x0, local copies, waits for them, and re-layouts: 47.6 us -> none  [one_mode(): state = lax.associative_scan(combine_pair, (factors, driven), axis=0)[1]]
    all_gather x1 -> x0, waiting for transfers between devices: 42.9 us -> none  [body(): piece = lax.all_gather(end_states[None], 'ctx', axis=0, tiled=True)]
    dynamic_update_slice x16 -> x0, local copies, waits for them, and re-layouts: 23.9 us -> none  [body(): local_part, end_states = lax.scan(one_mode, start, (rates, residues))]
    concatenate x96 -> x0, other arithmetic: 15.2 us -> none  [one_mode(): state = lax.associative_scan(combine_pair, (factors, driven), axis=0)[1]]
    ppermute x0 -> x7, starting transfers between devices: none -> 11.4 us  [the longest x3 5.65 us: shifted(): lax.ppermute(array, 'ctx', [(i, (i + 2 * by) % ctx) for i in range(ctx)])]
    pallas_call x0 -> x7, Pallas kernels: none -> 9.21 us  [call(): pl.pallas_call(kernel, out_shape=outputs, in_specs=specs, out_specs=out_s...]
  transfers between devices with their start and end apart: 1 -> 7, of which waited for: 1 -> 4; matrix products, arithmetic and copies ran while one was open for 0% -> 0% of each run, Pallas kernels for 0% -> 18%
where the time goes in v2:
time: 27.7 us; the launch traced here: 27.5 us
  starting transfers between devices  11.4 us (41%)
  Pallas kernels  9.21 us (33%)
  waiting for transfers between devices  6.49 us (23%)
    pallas_call x7, Pallas kernels, call(): pl.pallas_call(kernel, out_shape=outputs, in_specs=specs, out_specs=out_s...  9.21 us
    ppermute x3, starting transfers between devices, shifted(): lax.ppermute(array, 'ctx', [(i, (i + 2 * by) % ctx) for i in range(ctx)])  5.65 us
    ppermute x1, starting transfers between devices, body(): partner = lax.ppermute(other, 'ctx', pair)  3 us
    ppermute x2, waiting for transfers between devices, body(): lax.ppermute(parts[0], 'tp', [(i, i ^ mask) for i in range(tp)])  2.74 us
    ppermute x1, waiting for transfers between devices, body(): received = lax.ppermute(jnp.where(x == 0, second, before), 'ctx', pair)  2.04 us
    ppermute x3, waiting for transfers between devices, shifted(): lax.ppermute(array, 'ctx', [(i, (i + 2 * by) % ctx) for i in range(ctx)])  1.71 us
    ppermute x2, starting transfers between devices, body(): lax.ppermute(parts[0], 'tp', [(i, i ^ mask) for i in range(tp)])  1.4 us
    ppermute x1, starting transfers between devices, body(): received = lax.ppermute(jnp.where(x == 0, second, before), 'ctx', pair)  1.34 us
  transfers between devices with their start and end apart: 7, of which 4 were waited for; matrix products, arithmetic and copies ran while one was open for 0% of the time, Pallas kernels for 18%

profile of v2, /device:TPU:0, one launch (start us, length us, event | category | flops | bytes accessed | tf_op | source)
XLA Modules:
  0.0 27.5 jit_solution(3404388723788971234)
XLA Ops:
  0.0 0.0 copy-start
  0.0 2.1 %first_ends.1 = (f32[8,2048]{1,0:T(8,128)S(1)}, f32[128,2048]{1,0:T(8,128)S(1)}) custom-call(s32[1]{0:T(128)} %bitcast.refs_0_.x_ref, bf16[128,2048]{1,0:T(8,128)(2,1)} %refs_1_.1, bf16[128,2048]{1,0:T(8,128)(2,1)} %refs_2_.4, f32[16,2048]{1,0:T(8,128)} %refs_4_.1), custom_call_target="tpu_custom_call" | custom-call | flops 4194304 | bytes 2293764 | tf_op jit(solution)/shard_map/first_ends/pallas_call | solution.py:214
  2.1 3.0 %collective-permute-start = (f32[8,2048]{1,0:T(8,128)S(1)}, f32[8,2048]{1,0:T(8,128)S(1)}, u32[]{:S(2)}, u32[]{:S(2)}) collective-permute-start(f32[8,2048]{1,0:T(8,128)S(1)} %get-tuple-element.18), channel_id=1, source_target_pairs={{0,4},{4,0},{8,12},{12,8},{16,20},{20,16},{24,28},{28,24},{1,5},{5... | collective-permute-start | bytes 196616 | tf_op jit(solution)/shard_map/ppermute | solution.py:257
  5.1 0.0 copy-done
  5.1 0.0 copy-start.1
  5.1 0.0 copy-start.2
  5.1 0.0 copy-start.3
  5.1 0.8 %second_ends.1 = f32[8,2048]{1,0:T(8,128)S(1)} custom-call(s32[1]{0:T(128)} %bitcast.refs_0_.x_ref, f32[128,2048]{1,0:T(8,128)S(1)} %get-tuple-element.24.driven.refs_1_, f32[16,2048]{1,0:T(8,128)S(1)} %copy-done), custom_call_target="tpu_custom_call" | custom-call | flops 4194304 | bytes 1245188 | tf_op jit(solution)/shard_map/second_ends/pallas_call | solution.py:214
  6.0 0.2 copy-done.1
  6.2 0.0 copy-done.2
  6.2 0.0 copy-done.3
  6.2 1.6 %local_filter.2.refs_1_ = f32[128,1024]{1,0:T(8,128)S(1)} custom-call(bf16[128,2048]{1,0:T(8,128)(2,1)S(1)} %copy-done.1, f32[128,2048]{1,0:T(8,128)S(1)} %get-tuple-element.24.driven.refs_1_, f32[16,2048]{1,0:T(8,128)S(1)} %copy-done, f32[16,2048]{1,0:T(8,128)S(1)} %copy-done.2, f32[1,2048]{1,0:T(1,128)S(1)} %bitcast.3), custom_call_target="tpu_custom_call" | custom-call | flops 8388608 | bytes 2367488 | tf_op jit(solution)/shard_map/local_filter/pallas_call | solution.py:214
  7.8 0.0 collective-permute-done
  7.8 1.7 %collective-permute-start.3 = (f32[8,2048]{1,0:T(8,128)S(1)}, f32[8,2048]{1,0:T(8,128)S(1)}, u32[]{:S(2)}, u32[]{:S(2)}) collective-permute-start(f32[8,2048]{1,0:T(8,128)S(1)} %add_select_fusion), channel_id=1, source_target_pairs={{0,8},{4,12},{8,16},{12,20},{16,24},{20,28},{24,0},{28,4},{1,9},{5... | collective-permute-start | bytes 196616 | tf_op jit(solution)/shard_map/ppermute | solution.py:286
  9.6 2.6 %collective-permute-start.2 = (f32[8,2048]{1,0:T(8,128)S(1)}, f32[8,2048]{1,0:T(8,128)S(1)}, u32[]{:S(2)}, u32[]{:S(2)}) collective-permute-start(f32[8,2048]{1,0:T(8,128)S(1)} %add_select_fusion), channel_id=1, source_target_pairs={{0,16},{4,20},{8,24},{12,28},{16,0},{20,4},{24,8},{28,12},{1,17},{... | collective-permute-start | bytes 196616 | tf_op jit(solution)/shard_map/ppermute | solution.py:286
  12.2 1.3 %collective-permute-start.1 = (f32[8,2048]{1,0:T(8,128)S(1)}, f32[8,2048]{1,0:T(8,128)S(1)}, u32[]{:S(2)}, u32[]{:S(2)}) collective-permute-start(f32[8,2048]{1,0:T(8,128)S(1)} %add_select_fusion), channel_id=1, source_target_pairs={{0,24},{4,28},{8,0},{12,4},{16,8},{20,12},{24,16},{28,20},{1,25},{... | collective-permute-start | bytes 196616 | tf_op jit(solution)/shard_map/ppermute | solution.py:286
  13.5 1.6 %local_filter.3.refs_2_ = f32[128,1024]{1,0:T(8,128)S(1)} custom-call(bf16[128,2048]{1,0:T(8,128)(2,1)S(1)} %copy-done.1, f32[128,2048]{1,0:T(8,128)S(1)} %get-tuple-element.24.driven.refs_1_, f32[16,2048]{1,0:T(8,128)S(1)} %copy-done, f32[16,2048]{1,0:T(8,128)S(1)} %copy-done.2, f32[1,2048]{1,0:T(1,128)S(1)} %bitcast.4), custom_call_target="tpu_custom_call" | custom-call | flops 8388608 | bytes 2367488 | tf_op jit(solution)/shard_map/local_filter/pallas_call | solution.py:214
  15.1 0.0 collective-permute-done.3
  15.1 1.7 %collective-permute-done.2 = f32[8,2048]{1,0:T(8,128)S(1)} collective-permute-done((f32[8,2048]{1,0:T(8,128)S(1)}, f32[8,2048]{1,0:T(8,128)S(1)}, u32[]{:S(2)}, u32[]{:S(2)}) %collective-permute-start.2) | collective-permute-done | bytes 65568 | tf_op jit(solution)/shard_map/ppermute | solution.py:286
  16.8 0.0 collective-permute-done.1
  16.8 0.1 broadcast_select_fusion
  16.9 1.3 %collective-permute-start.4 = (f32[8,2048]{1,0:T(8,128)S(1)}, f32[8,2048]{1,0:T(8,128)S(1)}, u32[]{:S(2)}, u32[]{:S(2)}) collective-permute-start(f32[8,2048]{1,0:T(8,128)S(1)} %get-tuple-element.31), channel_id=1, source_target_pairs={{0,4},{4,0},{8,12},{12,8},{16,20},{20,16},{24,28},{28,24},{1,5},{5... | collective-permute-start | bytes 196616 | tf_op jit(solution)/shard_map/ppermute | solution.py:310
  18.2 0.9 %add_kept.1.refs_1_ = f32[128,2048]{1,0:T(8,128)S(1)} custom-call(s32[1]{0:T(128)} %bitcast.refs_0_.x_ref, f32[128,1024]{1,0:T(8,128)S(1)} %local_filter.2.refs_1_, f32[128,1024]{1,0:T(8,128)S(1)} %local_filter.3.refs_2_, bf16[128,2048]{1,0:T(8,128)(2,1)S(1)} %copy-done.1, f32[8,2048]{1,0:T(8,128)S(1)} %get-tuple-element.32.refs_4_, f32[16,2048]{1,0:T(8,128)S(1)} %copy-done, ...), custom_call_target="tpu_custom_call" | custom-call | flops 4194304 | bytes 2949124 | tf_op jit(solution)/shard_map/add_kept/pallas_call | solution.py:214
  19.2 2.0 %collective-permute-done.4.refs_3_ = f32[8,2048]{1,0:T(8,128)S(1)} collective-permute-done((f32[8,2048]{1,0:T(8,128)S(1)}, f32[8,2048]{1,0:T(8,128)S(1)}, u32[]{:S(2)}, u32[]{:S(2)}) %collective-permute-start.4) | collective-permute-done | bytes 65568 | tf_op jit(solution)/shard_map/ppermute | solution.py:310
  21.2 0.0 copy-start.4
  21.2 1.1 %add_received.1 = (f32[128,2048]{1,0:T(8,128)S(1)}, f32[1,128]{1,0:T(1,128)S(1)}) custom-call(s32[1]{0:T(128)} %bitcast.refs_0_.x_ref, f32[128,2048]{1,0:T(8,128)S(1)} %add_kept.1.refs_1_, bf16[128,2048]{1,0:T(8,128)(2,1)S(1)} %copy-done.1, f32[8,2048]{1,0:T(8,128)S(1)} %collective-permute-done.4.refs_3_, f32[16,2048]{1,0:T(8,128)S(1)} %copy-done, ...), custom_call_target="tpu_custom_call" | custom-call | flops 4194304 | bytes 2949636 | tf_op jit(solution)/shard_map/add_received/pallas_call | solution.py:214
  22.4 0.1 collective-permute-start.5
  22.5 1.1 %collective-permute-done.5 = f32[1,128]{1,0:T(1,128)S(1)} collective-permute-done((f32[1,128]{1,0:T(1,128)S(1)}, f32[1,128]{1,0:T(1,128)S(1)}, u32[]{:S(2)}, u32[]{:S(2)}) %collective-permute-start.5) | collective-permute-done | bytes 544 | tf_op jit(solution)/shard_map/ppermute | solution.py:338
  23.6 1.3 %collective-permute-start.6 = (f32[1,128]{1,0:T(1,128)S(1)}, f32[1,128]{1,0:T(1,128)S(1)}, u32[]{:S(2)}, u32[]{:S(2)}) collective-permute-start(f32[1,128]{1,0:T(1,128)S(1)} %add.29.refs_2_), channel_id=1, source_target_pairs={{0,3},{1,2},{2,1},{3,0},{4,7},{5,6},{6,5},{7,4},{8,11},{9,10},{10,... | collective-permute-start | bytes 1544 | tf_op jit(solution)/shard_map/ppermute | solution.py:338
  24.9 1.6 %collective-permute-done.6.refs_3_ = f32[1,128]{1,0:T(1,128)S(1)} collective-permute-done((f32[1,128]{1,0:T(1,128)S(1)}, f32[1,128]{1,0:T(1,128)S(1)}, u32[]{:S(2)}, u32[]{:S(2)}) %collective-permute-start.6) | collective-permute-done | bytes 544 | tf_op jit(solution)/shard_map/ppermute | solution.py:338
  26.5 0.0 copy-done.4
  26.5 1.0 %norm.1 = bf16[128,2048]{1,0:T(8,128)(2,1)} custom-call(f32[128,2048]{1,0:T(8,128)S(1)} %get-tuple-element.29.refs_0_, f32[1,2048]{1,0:T(1,128)S(1)} %bitcast.5, f32[1,128]{1,0:T(1,128)S(1)} %add.29.refs_2_, f32[1,128]{1,0:T(1,128)S(1)} %collective-permute-done.6.refs_3_), custom_call_target="tpu_custom_call" | custom-call | flops 524288 | bytes 1582080 | tf_op jit(solution)/shard_map/norm/pallas_call | solution.py:214
  (2 shorter events, 0.0 us)
Async XLA Ops:
  0.0 5.1 %copy-start = (f32[16,2048]{1,0:T(8,128)S(1)}, f32[16,2048]{1,0:T(8,128)}, u32[]{:S(2)}) copy-start(f32[16,2048]{1,0:T(8,128)} %refs_4_.1) | copy-start | bytes 393220
  2.1 5.7 %collective-permute-start = (f32[8,2048]{1,0:T(8,128)S(1)}, f32[8,2048]{1,0:T(8,128)S(1)}, u32[]{:S(2)}, u32[]{:S(2)}) collective-permute-start(f32[8,2048]{1,0:T(8,128)S(1)} %get-tuple-element.18), channel_id=1, source_target_pairs={{0,4},{4,0},{8,12},{12,8},{16,20},{20,16},{24,28},{28,24},{1,5},{5... | collective-permute-start | bytes 196616 | tf_op jit(solution)/shard_map/ppermute | solution.py:257
  5.1 1.0 %copy-start.1 = (bf16[128,2048]{1,0:T(8,128)(2,1)S(1)}, bf16[128,2048]{1,0:T(8,128)(2,1)}, u32[]{:S(2)}) copy-start(bf16[128,2048]{1,0:T(8,128)(2,1)} %refs_2_.7) | copy-start | bytes 1572868
  5.1 1.1 %copy-start.2 = (f32[16,2048]{1,0:T(8,128)S(1)}, f32[16,2048]{1,0:T(8,128)}, u32[]{:S(2)}) copy-start(f32[16,2048]{1,0:T(8,128)} %refs_5_.3) | copy-start | bytes 393220
  5.1 1.1 %copy-start.3 = (f32[2048]{0:T(1024)S(1)}, f32[2048]{0:T(1024)}, u32[]{:S(2)}) copy-start(f32[2048]{0:T(1024)} %param.12) | copy-start | bytes 24580
  7.8 7.3 %collective-permute-start.3 = (f32[8,2048]{1,0:T(8,128)S(1)}, f32[8,2048]{1,0:T(8,128)S(1)}, u32[]{:S(2)}, u32[]{:S(2)}) collective-permute-start(f32[8,2048]{1,0:T(8,128)S(1)} %add_select_fusion), channel_id=1, source_target_pairs={{0,8},{4,12},{8,16},{12,20},{16,24},{20,28},{24,0},{28,4},{1,9},{5... | collective-permute-start | bytes 196616 | tf_op jit(solution)/shard_map/ppermute | solution.py:286
  9.6 7.3 %collective-permute-start.2 = (f32[8,2048]{1,0:T(8,128)S(1)}, f32[8,2048]{1,0:T(8,128)S(1)}, u32[]{:S(2)}, u32[]{:S(2)}) collective-permute-start(f32[8,2048]{1,0:T(8,128)S(1)} %add_select_fusion), channel_id=1, source_target_pairs={{0,16},{4,20},{8,24},{12,28},{16,0},{20,4},{24,8},{28,12},{1,17},{... | collective-permute-start | bytes 196616 | tf_op jit(solution)/shard_map/ppermute | solution.py:286
  12.2 4.7 %collective-permute-start.1 = (f32[8,2048]{1,0:T(8,128)S(1)}, f32[8,2048]{1,0:T(8,128)S(1)}, u32[]{:S(2)}, u32[]{:S(2)}) collective-permute-start(f32[8,2048]{1,0:T(8,128)S(1)} %add_select_fusion), channel_id=1, source_target_pairs={{0,24},{4,28},{8,0},{12,4},{16,8},{20,12},{24,16},{28,20},{1,25},{... | collective-permute-start | bytes 196616 | tf_op jit(solution)/shard_map/ppermute | solution.py:286
  16.9 4.3 %collective-permute-start.4 = (f32[8,2048]{1,0:T(8,128)S(1)}, f32[8,2048]{1,0:T(8,128)S(1)}, u32[]{:S(2)}, u32[]{:S(2)}) collective-permute-start(f32[8,2048]{1,0:T(8,128)S(1)} %get-tuple-element.31), channel_id=1, source_target_pairs={{0,4},{4,0},{8,12},{12,8},{16,20},{20,16},{24,28},{28,24},{1,5},{5... | collective-permute-start | bytes 196616 | tf_op jit(solution)/shard_map/ppermute | solution.py:310
  21.2 5.3 %copy-start.4 = (f32[2048]{0:T(1024)S(1)}, f32[2048]{0:T(1024)}, u32[]{:S(2)}) copy-start(f32[2048]{0:T(1024)} %param.13) | copy-start | bytes 24580
  22.4 1.2 %collective-permute-start.5 = (f32[1,128]{1,0:T(1,128)S(1)}, f32[1,128]{1,0:T(1,128)S(1)}, u32[]{:S(2)}, u32[]{:S(2)}) collective-permute-start(f32[1,128]{1,0:T(1,128)S(1)} %get-tuple-element.30), channel_id=1, source_target_pairs={{0,1},{1,0},{2,3},{3,2},{4,5},{5,4},{6,7},{7,6},{8,9},{9,8},{10,11... | collective-permute-start | bytes 1544 | tf_op jit(solution)/shard_map/ppermute | solution.py:338
  23.6 3.0 %collective-permute-start.6 = (f32[1,128]{1,0:T(1,128)S(1)}, f32[1,128]{1,0:T(1,128)S(1)}, u32[]{:S(2)}, u32[]{:S(2)}) collective-permute-start(f32[1,128]{1,0:T(1,128)S(1)} %add.29.refs_2_), channel_id=1, source_target_pairs={{0,3},{1,2},{2,1},{3,0},{4,7},{5,6},{6,5},{7,4},{8,11},{9,10},{10,... | collective-permute-start | bytes 1544 | tf_op jit(solution)/shard_map/ppermute | solution.py:338

commit v3 on v2

--- a/solution.py
+++ b/solution.py
@@ -80,7 +80,7 @@
     for i in range(chunks):
         copies[2 * i].wait()
         copies[2 * i + 1].wait()
-        lax.fori_loop(i * groups, (i + 1) * groups, group_step, 0, unroll=min(2, groups))
+        lax.fori_loop(i * groups, (i + 1) * groups, group_step, 0, unroll=groups)
 
 
 def second_ends_kernel(x_ref, driven, rates, mine, decay, decay8, decay16, turn):
@@ -179,7 +179,7 @@
                     terms = [t * f for t, f in zip(terms, factors)]
             return unused
 
-        lax.fori_loop(0, groups, group_step, 0)
+        lax.fori_loop(0, groups, group_step, 0, unroll=4)
     if final:
         squares[...] = jnp.sum(jnp.transpose(sums[...]), axis=0, keepdims=True)
 
@@ -189,7 +189,7 @@
     count, width = gated.shape
     factor = lax.rsqrt(added(part[...] for part in sums) / C + 1e-06)
     factors[...] = jnp.transpose(jnp.broadcast_to(factor, (LANES, count)))
-    size = 2 * ROWS
+    size = 4 * ROWS
 
     def copy(i):
         rows = pl.ds(pl.multiple_of(i * size, size), size)
@@ -204,7 +204,7 @@
         copy(i).start()
         return unused
 
-    lax.fori_loop(0, count // size, chunk_step, 0)
+    lax.fori_loop(0, count // size, chunk_step, 0, unroll=count // size)
     for i in range(count // size):
         copy(i).wait()
 
@@ -238,7 +238,7 @@
     work = 2 * half * count * width
     pair = [(i, i ^ 1) for i in range(ctx)]
 
-    chunks = width // 256
+    chunks = 4
     other, driven = call(
         lambda *refs: first_ends_kernel(chunks, *refs),
         (x_ref, in_hbm(keys), in_hbm(values), in_hbm(rates)),
@@ -330,18 +330,9 @@
         name="add_received",
     )
 
-    parts = [squares]
-    if tp & (tp - 1) == 0:
-        mask = 1
-        while mask < tp:
-            parts = [added(parts)]
-            parts.append(lax.ppermute(parts[0], "tp", [(i, i ^ mask) for i in range(tp)]))
-            mask = 2 * mask + 1
-    else:
-        total = squares
-        for by in range(1, tp):
-            total = total + lax.ppermute(squares, "tp", [(i, (i + by) % tp) for i in range(tp)])
-        parts = [total]
+    parts = [squares] + [
+        lax.ppermute(squares, "tp", [(i, i ^ by) for i in range(tp)]) for by in (1, 2, 3)
+    ]
     (out,) = call(
         lambda *refs: norm_kernel(len(parts), *refs),
         (gated, gain[None], *parts),
@@ -351,7 +342,7 @@
         scratch=[
             vmem(count, LANES),
             pltpu.VMEM((count, width), query.dtype),
-            pltpu.SemaphoreType.DMA((count // (2 * ROWS),)),
+            pltpu.SemaphoreType.DMA((count // (4 * ROWS),)),
         ],
         flops=2 * count * width,
         name="norm",

time: 27.7 us -> 26.9 us (0.971)
  waiting for transfers between devices: 6.49 us -> 5.63 us
  starting transfers between devices: 11.4 us -> 11.9 us
  Pallas kernels: 9.21 us -> 8.74 us
    ppermute x2 -> x3, waiting for transfers between devices: 2.74 us -> 1.76 us  [body(): lax.ppermute(squares, 'tp', [(i, i ^ by) for i in range(tp)])]
    ppermute x2 -> x3, starting transfers between devices: 1.4 us -> 1.92 us  [body(): lax.ppermute(squares, 'tp', [(i, i ^ by) for i in range(tp)])]
    pallas_call x7, Pallas kernels: 9.21 us -> 8.74 us  [call(): pl.pallas_call(kernel, out_shape=outputs, in_specs=specs, out_specs=out_s...]
  transfers between devices with their start and end apart: 7 -> 8, of which waited for: 4 -> 4; matrix products, arithmetic and copies ran while one was open for 0% -> 0% of each run, Pallas kernels for 18% -> 18%
where the time goes in v3:
time: 26.9 us; the launch traced here: 26.7 us
  starting transfers between devices  11.9 us (44%)
  Pallas kernels  8.74 us (32%)
  waiting for transfers between devices  5.63 us (21%)
    pallas_call x7, Pallas kernels, call(): pl.pallas_call(kernel, out_shape=outputs, in_specs=specs, out_specs=out_s...  8.74 us
    ppermute x3, starting transfers between devices, shifted(): lax.ppermute(array, 'ctx', [(i, (i + 2 * by) % ctx) for i in range(ctx)])  5.65 us
    ppermute x1, starting transfers between devices, body(): partner = lax.ppermute(other, 'ctx', pair)  3 us
    ppermute x1, waiting for transfers between devices, body(): received = lax.ppermute(jnp.where(x == 0, second, before), 'ctx', pair)  2.16 us
    ppermute x3, starting transfers between devices, body(): lax.ppermute(squares, 'tp', [(i, i ^ by) for i in range(tp)])  1.92 us
    ppermute x3, waiting for transfers between devices, body(): lax.ppermute(squares, 'tp', [(i, i ^ by) for i in range(tp)])  1.76 us
    ppermute x3, waiting for transfers between devices, shifted(): lax.ppermute(array, 'ctx', [(i, (i + 2 * by) % ctx) for i in range(ctx)])  1.71 us
    ppermute x1, starting transfers between devices, body(): received = lax.ppermute(jnp.where(x == 0, second, before), 'ctx', pair)  1.34 us
  transfers between devices with their start and end apart: 8, of which 4 were waited for; matrix products, arithmetic and copies ran while one was open for 0% of the time, Pallas kernels for 18%

profile of v3, /device:TPU:0, one launch (start us, length us, event | category | flops | bytes accessed | tf_op | source)
XLA Modules:
  0.0 26.7 jit_solution(15894675440842563153)
XLA Ops:
  0.0 0.0 copy-start
  0.0 2.0 %first_ends.1 = (f32[8,2048]{1,0:T(8,128)S(1)}, f32[128,2048]{1,0:T(8,128)S(1)}) custom-call(s32[1]{0:T(128)} %bitcast.refs_0_.x_ref, bf16[128,2048]{1,0:T(8,128)(2,1)} %refs_1_.1, bf16[128,2048]{1,0:T(8,128)(2,1)} %refs_2_.4, f32[16,2048]{1,0:T(8,128)} %refs_4_.1), custom_call_target="tpu_custom_call" | custom-call | flops 4194304 | bytes 2293764 | tf_op jit(solution)/shard_map/first_ends/pallas_call | solution.py:214
  2.0 3.0 %collective-permute-start = (f32[8,2048]{1,0:T(8,128)S(1)}, f32[8,2048]{1,0:T(8,128)S(1)}, u32[]{:S(2)}, u32[]{:S(2)}) collective-permute-start(f32[8,2048]{1,0:T(8,128)S(1)} %get-tuple-element.18), channel_id=1, source_target_pairs={{0,4},{4,0},{8,12},{12,8},{16,20},{20,16},{24,28},{28,24},{1,5},{5... | collective-permute-start | bytes 196616 | tf_op jit(solution)/shard_map/ppermute | solution.py:257
  5.0 0.0 copy-done
  5.0 0.0 copy-start.1
  5.0 0.0 copy-start.2
  5.0 0.8 %second_ends.1 = f32[8,2048]{1,0:T(8,128)S(1)} custom-call(s32[1]{0:T(128)} %bitcast.refs_0_.x_ref, f32[128,2048]{1,0:T(8,128)S(1)} %get-tuple-element.24.driven.refs_1_, f32[16,2048]{1,0:T(8,128)S(1)} %copy-done), custom_call_target="tpu_custom_call" | custom-call | flops 4194304 | bytes 1245188 | tf_op jit(solution)/shard_map/second_ends/pallas_call | solution.py:214
  5.8 0.2 copy-done.1
  6.0 0.0 copy-done.2
  6.0 0.0 copy-done.3
  6.0 1.6 %local_filter.2.refs_1_ = f32[128,1024]{1,0:T(8,128)S(1)} custom-call(bf16[128,2048]{1,0:T(8,128)(2,1)S(1)} %copy-done.1, f32[128,2048]{1,0:T(8,128)S(1)} %get-tuple-element.24.driven.refs_1_, f32[16,2048]{1,0:T(8,128)S(1)} %copy-done, f32[16,2048]{1,0:T(8,128)S(1)} %copy-done.2, f32[1,2048]{1,0:T(1,128)S(1)} %bitcast.3), custom_call_target="tpu_custom_call" | custom-call | flops 8388608 | bytes 2367488 | tf_op jit(solution)/shard_map/local_filter/pallas_call | solution.py:214
  7.7 0.0 collective-permute-done
  7.7 1.7 %collective-permute-start.3 = (f32[8,2048]{1,0:T(8,128)S(1)}, f32[8,2048]{1,0:T(8,128)S(1)}, u32[]{:S(2)}, u32[]{:S(2)}) collective-permute-start(f32[8,2048]{1,0:T(8,128)S(1)} %add_select_fusion), channel_id=1, source_target_pairs={{0,8},{4,12},{8,16},{12,20},{16,24},{20,28},{24,0},{28,4},{1,9},{5... | collective-permute-start | bytes 196616 | tf_op jit(solution)/shard_map/ppermute | solution.py:286
  9.4 2.6 %collective-permute-start.2 = (f32[8,2048]{1,0:T(8,128)S(1)}, f32[8,2048]{1,0:T(8,128)S(1)}, u32[]{:S(2)}, u32[]{:S(2)}) collective-permute-start(f32[8,2048]{1,0:T(8,128)S(1)} %add_select_fusion), channel_id=1, source_target_pairs={{0,16},{4,20},{8,24},{12,28},{16,0},{20,4},{24,8},{28,12},{1,17},{... | collective-permute-start | bytes 196616 | tf_op jit(solution)/shard_map/ppermute | solution.py:286
  12.0 1.3 %collective-permute-start.1 = (f32[8,2048]{1,0:T(8,128)S(1)}, f32[8,2048]{1,0:T(8,128)S(1)}, u32[]{:S(2)}, u32[]{:S(2)}) collective-permute-start(f32[8,2048]{1,0:T(8,128)S(1)} %add_select_fusion), channel_id=1, source_target_pairs={{0,24},{4,28},{8,0},{12,4},{16,8},{20,12},{24,16},{28,20},{1,25},{... | collective-permute-start | bytes 196616 | tf_op jit(solution)/shard_map/ppermute | solution.py:286
  13.4 1.6 %local_filter.3.refs_2_ = f32[128,1024]{1,0:T(8,128)S(1)} custom-call(bf16[128,2048]{1,0:T(8,128)(2,1)S(1)} %copy-done.1, f32[128,2048]{1,0:T(8,128)S(1)} %get-tuple-element.24.driven.refs_1_, f32[16,2048]{1,0:T(8,128)S(1)} %copy-done, f32[16,2048]{1,0:T(8,128)S(1)} %copy-done.2, f32[1,2048]{1,0:T(1,128)S(1)} %bitcast.4), custom_call_target="tpu_custom_call" | custom-call | flops 8388608 | bytes 2367488 | tf_op jit(solution)/shard_map/local_filter/pallas_call | solution.py:214
  15.0 0.0 collective-permute-done.3
  15.0 1.7 %collective-permute-done.2 = f32[8,2048]{1,0:T(8,128)S(1)} collective-permute-done((f32[8,2048]{1,0:T(8,128)S(1)}, f32[8,2048]{1,0:T(8,128)S(1)}, u32[]{:S(2)}, u32[]{:S(2)}) %collective-permute-start.2) | collective-permute-done | bytes 65568 | tf_op jit(solution)/shard_map/ppermute | solution.py:286
  16.7 0.0 collective-permute-done.1
  16.7 0.1 broadcast_select_fusion
  16.8 1.3 %collective-permute-start.4 = (f32[8,2048]{1,0:T(8,128)S(1)}, f32[8,2048]{1,0:T(8,128)S(1)}, u32[]{:S(2)}, u32[]{:S(2)}) collective-permute-start(f32[8,2048]{1,0:T(8,128)S(1)} %get-tuple-element.31), channel_id=1, source_target_pairs={{0,4},{4,0},{8,12},{12,8},{16,20},{20,16},{24,28},{28,24},{1,5},{5... | collective-permute-start | bytes 196616 | tf_op jit(solution)/shard_map/ppermute | solution.py:310
  18.1 0.8 %add_kept.1.refs_1_ = f32[128,2048]{1,0:T(8,128)S(1)} custom-call(s32[1]{0:T(128)} %bitcast.refs_0_.x_ref, f32[128,1024]{1,0:T(8,128)S(1)} %local_filter.2.refs_1_, f32[128,1024]{1,0:T(8,128)S(1)} %local_filter.3.refs_2_, bf16[128,2048]{1,0:T(8,128)(2,1)S(1)} %copy-done.1, f32[8,2048]{1,0:T(8,128)S(1)} %get-tuple-element.32.refs_4_, f32[16,2048]{1,0:T(8,128)S(1)} %copy-done, ...), custom_call_target="tpu_custom_call" | custom-call | flops 4194304 | bytes 2949124 | tf_op jit(solution)/shard_map/add_kept/pallas_call | solution.py:214
  18.9 2.2 %collective-permute-done.4.refs_3_ = f32[8,2048]{1,0:T(8,128)S(1)} collective-permute-done((f32[8,2048]{1,0:T(8,128)S(1)}, f32[8,2048]{1,0:T(8,128)S(1)}, u32[]{:S(2)}, u32[]{:S(2)}) %collective-permute-start.4) | collective-permute-done | bytes 65568 | tf_op jit(solution)/shard_map/ppermute | solution.py:310
  21.1 1.0 %add_received.1 = (f32[128,2048]{1,0:T(8,128)S(1)}, f32[1,128]{1,0:T(1,128)S(1)}) custom-call(s32[1]{0:T(128)} %bitcast.refs_0_.x_ref, f32[128,2048]{1,0:T(8,128)S(1)} %add_kept.1.refs_1_, bf16[128,2048]{1,0:T(8,128)(2,1)S(1)} %copy-done.1, f32[8,2048]{1,0:T(8,128)S(1)} %collective-permute-done.4.refs_3_, f32[16,2048]{1,0:T(8,128)S(1)} %copy-done, ...), custom_call_target="tpu_custom_call" | custom-call | flops 4194304 | bytes 2949636 | tf_op jit(solution)/shard_map/add_received/pallas_call | solution.py:214
  22.1 0.1 collective-permute-start.7
  22.2 1.6 %collective-permute-start.6 = (f32[1,128]{1,0:T(1,128)S(1)}, f32[1,128]{1,0:T(1,128)S(1)}, u32[]{:S(2)}, u32[]{:S(2)}) collective-permute-start(f32[1,128]{1,0:T(1,128)S(1)} %get-tuple-element.30.refs_2_), channel_id=1, source_target_pairs={{0,2},{1,3},{2,0},{3,1},{4,6},{5,7},{6,4},{7,5},{8,10},{9,11},{10,... | collective-permute-start | bytes 1544 | tf_op jit(solution)/shard_map/ppermute | solution.py:334
  23.8 0.3 collective-permute-start.5
  24.0 1.1 %collective-permute-done.7.refs_5_ = f32[1,128]{1,0:T(1,128)S(1)} collective-permute-done((f32[1,128]{1,0:T(1,128)S(1)}, f32[1,128]{1,0:T(1,128)S(1)}, u32[]{:S(2)}, u32[]{:S(2)}) %collective-permute-start.7) | collective-permute-done | bytes 544 | tf_op jit(solution)/shard_map/ppermute | solution.py:334
  25.1 0.7 %collective-permute-done.6.refs_4_ = f32[1,128]{1,0:T(1,128)S(1)} collective-permute-done((f32[1,128]{1,0:T(1,128)S(1)}, f32[1,128]{1,0:T(1,128)S(1)}, u32[]{:S(2)}, u32[]{:S(2)}) %collective-permute-start.6) | collective-permute-done | bytes 544 | tf_op jit(solution)/shard_map/ppermute | solution.py:334
  25.8 0.0 collective-permute-done.5.refs_3_
  25.8 0.0 copy-done.4
  25.8 0.9 %norm.1 = bf16[128,2048]{1,0:T(8,128)(2,1)} custom-call(f32[128,2048]{1,0:T(8,128)S(1)} %get-tuple-element.29.refs_0_, f32[1,2048]{1,0:T(1,128)S(1)} %bitcast.5, f32[1,128]{1,0:T(1,128)S(1)} %get-tuple-element.30.refs_2_, f32[1,128]{1,0:T(1,128)S(1)} %collective-permute-done.5.refs_3_, f32[1,128]{1,0:T(1,128)S(1)} %collective-permute-done.6.refs_4_, ...), custom_call_target="tpu_custom_call" | custom-call | flops 524288 | bytes 1583104 | tf_op jit(solution)/shard_map/norm/pallas_call | solution.py:214
  (3 shorter events, 0.0 us)
Async XLA Ops:
  0.0 5.0 %copy-start = (f32[16,2048]{1,0:T(8,128)S(1)}, f32[16,2048]{1,0:T(8,128)}, u32[]{:S(2)}) copy-start(f32[16,2048]{1,0:T(8,128)} %refs_4_.1) | copy-start | bytes 393220
  2.0 5.7 %collective-permute-start = (f32[8,2048]{1,0:T(8,128)S(1)}, f32[8,2048]{1,0:T(8,128)S(1)}, u32[]{:S(2)}, u32[]{:S(2)}) collective-permute-start(f32[8,2048]{1,0:T(8,128)S(1)} %get-tuple-element.18), channel_id=1, source_target_pairs={{0,4},{4,0},{8,12},{12,8},{16,20},{20,16},{24,28},{28,24},{1,5},{5... | collective-permute-start | bytes 196616 | tf_op jit(solution)/shard_map/ppermute | solution.py:257
  5.0 1.0 %copy-start.1 = (bf16[128,2048]{1,0:T(8,128)(2,1)S(1)}, bf16[128,2048]{1,0:T(8,128)(2,1)}, u32[]{:S(2)}) copy-start(bf16[128,2048]{1,0:T(8,128)(2,1)} %refs_2_.7) | copy-start | bytes 1572868
  5.0 1.1 %copy-start.2 = (f32[16,2048]{1,0:T(8,128)S(1)}, f32[16,2048]{1,0:T(8,128)}, u32[]{:S(2)}) copy-start(f32[16,2048]{1,0:T(8,128)} %refs_5_.3) | copy-start | bytes 393220
  5.0 1.1 %copy-start.3 = (f32[2048]{0:T(1024)S(1)}, f32[2048]{0:T(1024)}, u32[]{:S(2)}) copy-start(f32[2048]{0:T(1024)} %param.12) | copy-start | bytes 24580
  7.7 7.3 %collective-permute-start.3 = (f32[8,2048]{1,0:T(8,128)S(1)}, f32[8,2048]{1,0:T(8,128)S(1)}, u32[]{:S(2)}, u32[]{:S(2)}) collective-permute-start(f32[8,2048]{1,0:T(8,128)S(1)} %add_select_fusion), channel_id=1, source_target_pairs={{0,8},{4,12},{8,16},{12,20},{16,24},{20,28},{24,0},{28,4},{1,9},{5... | collective-permute-start | bytes 196616 | tf_op jit(solution)/shard_map/ppermute | solution.py:286
  9.4 7.3 %collective-permute-start.2 = (f32[8,2048]{1,0:T(8,128)S(1)}, f32[8,2048]{1,0:T(8,128)S(1)}, u32[]{:S(2)}, u32[]{:S(2)}) collective-permute-start(f32[8,2048]{1,0:T(8,128)S(1)} %add_select_fusion), channel_id=1, source_target_pairs={{0,16},{4,20},{8,24},{12,28},{16,0},{20,4},{24,8},{28,12},{1,17},{... | collective-permute-start | bytes 196616 | tf_op jit(solution)/shard_map/ppermute | solution.py:286
  12.0 4.7 %collective-permute-start.1 = (f32[8,2048]{1,0:T(8,128)S(1)}, f32[8,2048]{1,0:T(8,128)S(1)}, u32[]{:S(2)}, u32[]{:S(2)}) collective-permute-start(f32[8,2048]{1,0:T(8,128)S(1)} %add_select_fusion), channel_id=1, source_target_pairs={{0,24},{4,28},{8,0},{12,4},{16,8},{20,12},{24,16},{28,20},{1,25},{... | collective-permute-start | bytes 196616 | tf_op jit(solution)/shard_map/ppermute | solution.py:286
  16.8 4.3 %collective-permute-start.4 = (f32[8,2048]{1,0:T(8,128)S(1)}, f32[8,2048]{1,0:T(8,128)S(1)}, u32[]{:S(2)}, u32[]{:S(2)}) collective-permute-start(f32[8,2048]{1,0:T(8,128)S(1)} %get-tuple-element.31), channel_id=1, source_target_pairs={{0,4},{4,0},{8,12},{12,8},{16,20},{20,16},{24,28},{28,24},{1,5},{5... | collective-permute-start | bytes 196616 | tf_op jit(solution)/shard_map/ppermute | solution.py:310
  21.1 4.7 %copy-start.4 = (f32[2048]{0:T(1024)S(1)}, f32[2048]{0:T(1024)}, u32[]{:S(2)}) copy-start(f32[2048]{0:T(1024)} %param.13) | copy-start | bytes 24580
  22.1 3.0 %collective-permute-start.7 = (f32[1,128]{1,0:T(1,128)S(1)}, f32[1,128]{1,0:T(1,128)S(1)}, u32[]{:S(2)}, u32[]{:S(2)}) collective-permute-start(f32[1,128]{1,0:T(1,128)S(1)} %get-tuple-element.30.refs_2_), channel_id=1, source_target_pairs={{0,3},{1,2},{2,1},{3,0},{4,7},{5,6},{6,5},{7,4},{8,11},{9,10},{10,... | collective-permute-start | bytes 1544 | tf_op jit(solution)/shard_map/ppermute | solution.py:334
  22.2 3.6 %collective-permute-start.6 = (f32[1,128]{1,0:T(1,128)S(1)}, f32[1,128]{1,0:T(1,128)S(1)}, u32[]{:S(2)}, u32[]{:S(2)}) collective-permute-start(f32[1,128]{1,0:T(1,128)S(1)} %get-tuple-element.30.refs_2_), channel_id=1, source_target_pairs={{0,2},{1,3},{2,0},{3,1},{4,6},{5,7},{6,4},{7,5},{8,10},{9,11},{10,... | collective-permute-start | bytes 1544 | tf_op jit(solution)/shard_map/ppermute | solution.py:334
  23.8 2.0 %collective-permute-start.5 = (f32[1,128]{1,0:T(1,128)S(1)}, f32[1,128]{1,0:T(1,128)S(1)}, u32[]{:S(2)}, u32[]{:S(2)}) collective-permute-start(f32[1,128]{1,0:T(1,128)S(1)} %get-tuple-element.30.refs_2_), channel_id=1, source_target_pairs={{0,1},{1,0},{2,3},{3,2},{4,5},{5,4},{6,7},{7,6},{8,9},{9,8},{10,11... | collective-permute-start | bytes 1544 | tf_op jit(solution)/shard_map/ppermute | solution.py:334

commit v4 on v3

--- a/solution.py
+++ b/solution.py
@@ -290,20 +290,46 @@
     pair_state = jnp.where(x == 0, mine * step + partner, partner * step + mine)
     pair_state, driven = tied((pair_state, driven))
 
-    span = min(3, outer - 1)
-    moved = [shifted(pair_state, by) for by in range(span, 0, -1)]
-    late = [local_part(part, driven) for part in range(pieces // 2, pieces)]
-    moved, late = tied((moved, late))
-    before = jnp.zeros_like(mine)
-    for by, states in zip(range(span, 0, -1), moved):
-        weight = jnp.exp(-my_rates * (2 * count * (by - 1)))
-        before = before + jnp.where(z >= by, weight * states, 0.0)
-    while span < outer - 1:
-        moved = [(by, shifted(before, by)) for by in range(3 * span, 0, -span) if by < outer]
-        for by, states in moved:
-            weight = jnp.exp(-my_rates * (2 * count * by))
+    def late_parts():
+        return [local_part(part, driven) for part in range(pieces // 2, pieces)]
+
+    if outer == 4 and tp % 2 == 0:
+        def moved(array, targets):
+            def target(i, j):
+                to = targets[i // 2]
+                return (2 * to + i % 2) * tp + (j if to != i // 2 else j ^ 1)
+
+            links = [(i * tp + j, target(i, j)) for i in range(ctx) for j in range(tp)]
+            return lax.ppermute(array, ("ctx", "tp"), links)
+
+        span = jnp.exp(-my_rates * (2 * count))
+        first_move = moved(pair_state, (1, 2, 0, 3))
+        second_move = moved(pair_state, (0, 1, 3, 2))
+        third_move = moved(pair_state, (2, 1, 0, 3))
+        late = late_parts()
+        first_move, late = tied((first_move, late))
+        both = jnp.where(z == 1, span * first_move + pair_state, pair_state)
+        handed = moved(both, (0, 3, 1, 2))
+        before = jnp.where(
+            z == 0,
+            0.0,
+            jnp.where(z == 1, first_move, jnp.where(z == 2, first_move + span * third_move, second_move + span * handed)),
+        )
+    else:
+        span = min(3, outer - 1)
+        parts = [shifted(pair_state, by) for by in range(span, 0, -1)]
+        late = late_parts()
+        parts, late = tied((parts, late))
+        before = jnp.zeros_like(mine)
+        for by, states in zip(range(span, 0, -1), parts):
+            weight = jnp.exp(-my_rates * (2 * count * (by - 1)))
             before = before + jnp.where(z >= by, weight * states, 0.0)
-        span = 4 * span
+        while span < outer - 1:
+            parts = [(by, shifted(before, by)) for by in range(3 * span, 0, -span) if by < outer]
+            for by, states in parts:
+                weight = jnp.exp(-my_rates * (2 * count * by))
+                before = before + jnp.where(z >= by, weight * states, 0.0)
+            span = 4 * span
 
     second = before * step + jnp.where(x == 0, mine, partner)
     kept = jnp.where(x == 0, before, second)

time: 26.9 us -> 25.7 us (0.955)
  the two profiles are of different devices: /device:TPU:0 before, /device:TPU:17 now
where the time goes in v4:
time: 25.7 us; the launch traced here: 25.6 us
  starting transfers between devices  10.4 us (40%)
  Pallas kernels  8.75 us (34%)
  waiting for transfers between devices  5.97 us (23%)
    pallas_call x7, Pallas kernels, call(): pl.pallas_call(kernel, out_shape=outputs, in_specs=specs, out_specs=out_s...  8.75 us
    ppermute x3, starting transfers between devices, body(): lax.ppermute(squares, 'tp', [(i, i ^ by) for i in range(tp)])  4.96 us
    ppermute x4, waiting for transfers between devices, moved(): return lax.ppermute(array, ('ctx', 'tp'), links)  3.01 us
    ppermute x4, starting transfers between devices, moved(): return lax.ppermute(array, ('ctx', 'tp'), links)  2.88 us
    ppermute x3, waiting for transfers between devices, body(): lax.ppermute(squares, 'tp', [(i, i ^ by) for i in range(tp)])  1.92 us
    ppermute x1, starting transfers between devices, body(): partner = lax.ppermute(other, 'ctx', pair)  1.28 us
    ppermute x1, starting transfers between devices, body(): received = lax.ppermute(jnp.where(x == 0, second, before), 'ctx', pair)  1.28 us
    ppermute x1, waiting for transfers between devices, body(): received = lax.ppermute(jnp.where(x == 0, second, before), 'ctx', pair)  1.04 us
  transfers between devices with their start and end apart: 9, of which 5 were waited for; matrix products, arithmetic and copies ran while one was open for 0% of the time, Pallas kernels for 19%

profile of v4, /device:TPU:17, one launch (start us, length us, event | category | flops | bytes accessed | tf_op | source)
XLA Modules:
  0.0 25.6 jit_solution(13940805926447851847)
XLA Ops:
  0.0 2.0 %first_ends.1 = (f32[8,2048]{1,0:T(8,128)S(1)}, f32[128,2048]{1,0:T(8,128)S(1)}) custom-call(s32[1]{0:T(128)} %bitcast.refs_0_.x_ref, bf16[128,2048]{1,0:T(8,128)(2,1)} %refs_1_.1, bf16[128,2048]{1,0:T(8,128)(2,1)} %refs_2_.4, f32[16,2048]{1,0:T(8,128)} %refs_4_.1), custom_call_target="tpu_custom_call" | custom-call | flops 4194304 | bytes 2293764 | tf_op jit(solution)/shard_map/first_ends/pallas_call | solution.py:214
  2.0 1.3 %collective-permute-start = (f32[8,2048]{1,0:T(8,128)S(1)}, f32[8,2048]{1,0:T(8,128)S(1)}, u32[]{:S(2)}, u32[]{:S(2)}) collective-permute-start(f32[8,2048]{1,0:T(8,128)S(1)} %get-tuple-element.16), channel_id=1, source_target_pairs={{0,4},{4,0},{8,12},{12,8},{16,20},{20,16},{24,28},{28,24},{1,5},{5... | collective-permute-start | bytes 196616 | tf_op jit(solution)/shard_map/ppermute | solution.py:257
  3.2 0.0 copy-done.1
  3.3 0.0 copy-start
  3.3 0.0 copy-start.2
  3.3 0.8 %second_ends.1 = f32[8,2048]{1,0:T(8,128)S(1)} custom-call(s32[1]{0:T(128)} %bitcast.refs_0_.x_ref, f32[128,2048]{1,0:T(8,128)S(1)} %get-tuple-element.22.driven.refs_1_, f32[16,2048]{1,0:T(8,128)S(1)} %copy-done.1), custom_call_target="tpu_custom_call" | custom-call | flops 4194304 | bytes 1245188 | tf_op jit(solution)/shard_map/second_ends/pallas_call | solution.py:214
  4.1 0.2 copy-done
  4.3 0.0 copy-done.2
  4.3 0.0 copy-done.3
  4.3 1.6 %local_filter.2.refs_1_ = f32[128,1024]{1,0:T(8,128)S(1)} custom-call(bf16[128,2048]{1,0:T(8,128)(2,1)S(1)} %copy-done, f32[128,2048]{1,0:T(8,128)S(1)} %get-tuple-element.22.driven.refs_1_, f32[16,2048]{1,0:T(8,128)S(1)} %copy-done.1, f32[16,2048]{1,0:T(8,128)S(1)} %copy-done.2, f32[1,2048]{1,0:T(1,128)S(1)} %bitcast.3), custom_call_target="tpu_custom_call" | custom-call | flops 8388608 | bytes 2367488 | tf_op jit(solution)/shard_map/local_filter/pallas_call | solution.py:214
  5.9 0.0 collective-permute-done
  6.0 0.1 collective-permute-start.1
  6.1 2.3 %collective-permute-start.3 = (f32[8,2048]{1,0:T(8,128)S(1)}, f32[8,2048]{1,0:T(8,128)S(1)}, u32[]{:S(2)}, u32[]{:S(2)}) collective-permute-start(f32[8,2048]{1,0:T(8,128)S(1)} %get-tuple-element.21), channel_id=1, source_target_pairs={{0,1},{1,0},{2,3},{3,2},{4,5},{5,4},{6,7},{7,6},{8,9},{9,8},{10,11... | collective-permute-start | bytes 196616 | tf_op jit(solution)/shard_map/ppermute | solution.py:303
  8.4 0.3 %collective-permute-start.2 = (f32[8,2048]{1,0:T(8,128)S(1)}, f32[8,2048]{1,0:T(8,128)S(1)}, u32[]{:S(2)}, u32[]{:S(2)}) collective-permute-start(f32[8,2048]{1,0:T(8,128)S(1)} %get-tuple-element.21), channel_id=1, source_target_pairs={{0,16},{1,17},{2,18},{3,19},{4,20},{5,21},{6,22},{7,23},{8,9},{9,8... | collective-permute-start | bytes 196616 | tf_op jit(solution)/shard_map/ppermute | solution.py:303
  8.7 1.6 %local_filter.3.refs_2_ = f32[128,1024]{1,0:T(8,128)S(1)} custom-call(bf16[128,2048]{1,0:T(8,128)(2,1)S(1)} %copy-done, f32[128,2048]{1,0:T(8,128)S(1)} %get-tuple-element.22.driven.refs_1_, f32[16,2048]{1,0:T(8,128)S(1)} %copy-done.1, f32[16,2048]{1,0:T(8,128)S(1)} %copy-done.2, f32[1,2048]{1,0:T(1,128)S(1)} %bitcast.4), custom_call_target="tpu_custom_call" | custom-call | flops 8388608 | bytes 2367488 | tf_op jit(solution)/shard_map/local_filter/pallas_call | solution.py:214
  10.3 0.0 collective-permute-done.1
  10.4 0.2 collective-permute-start.4
  10.5 0.0 collective-permute-done.3
  10.5 1.9 %collective-permute-done.2 = f32[8,2048]{1,0:T(8,128)S(1)} collective-permute-done((f32[8,2048]{1,0:T(8,128)S(1)}, f32[8,2048]{1,0:T(8,128)S(1)}, u32[]{:S(2)}, u32[]{:S(2)}) %collective-permute-start.2) | collective-permute-done | bytes 65568 | tf_op jit(solution)/shard_map/ppermute | solution.py:303
  12.4 1.1 %collective-permute-done.4 = f32[8,2048]{1,0:T(8,128)S(1)} collective-permute-done((f32[8,2048]{1,0:T(8,128)S(1)}, f32[8,2048]{1,0:T(8,128)S(1)}, u32[]{:S(2)}, u32[]{:S(2)}) %collective-permute-start.4) | collective-permute-done | bytes 65568 | tf_op jit(solution)/shard_map/ppermute | solution.py:303
  13.6 1.3 %collective-permute-start.5 = (f32[8,2048]{1,0:T(8,128)S(1)}, f32[8,2048]{1,0:T(8,128)S(1)}, u32[]{:S(2)}, u32[]{:S(2)}) collective-permute-start(f32[8,2048]{1,0:T(8,128)S(1)} %get-tuple-element.27), channel_id=1, source_target_pairs={{0,4},{4,0},{8,12},{12,8},{16,20},{20,16},{24,28},{28,24},{1,5},{5... | collective-permute-start | bytes 196616 | tf_op jit(solution)/shard_map/ppermute | solution.py:336
  14.9 0.8 %add_kept.1.refs_1_ = f32[128,2048]{1,0:T(8,128)S(1)} custom-call(s32[1]{0:T(128)} %bitcast.refs_0_.x_ref, f32[128,1024]{1,0:T(8,128)S(1)} %local_filter.2.refs_1_, f32[128,1024]{1,0:T(8,128)S(1)} %local_filter.3.refs_2_, bf16[128,2048]{1,0:T(8,128)(2,1)S(1)} %copy-done, f32[8,2048]{1,0:T(8,128)S(1)} %broadcast_select_fusion.1.refs_4_, ...), custom_call_target="tpu_custom_call" | custom-call | flops 4194304 | bytes 2949124 | tf_op jit(solution)/shard_map/add_kept/pallas_call | solution.py:214
  15.7 1.0 %collective-permute-done.5.refs_3_ = f32[8,2048]{1,0:T(8,128)S(1)} collective-permute-done((f32[8,2048]{1,0:T(8,128)S(1)}, f32[8,2048]{1,0:T(8,128)S(1)}, u32[]{:S(2)}, u32[]{:S(2)}) %collective-permute-start.5) | collective-permute-done | bytes 65568 | tf_op jit(solution)/shard_map/ppermute | solution.py:336
  16.8 1.0 %add_received.1 = (f32[128,2048]{1,0:T(8,128)S(1)}, f32[1,128]{1,0:T(1,128)S(1)}) custom-call(s32[1]{0:T(128)} %bitcast.refs_0_.x_ref, f32[128,2048]{1,0:T(8,128)S(1)} %add_kept.1.refs_1_, bf16[128,2048]{1,0:T(8,128)(2,1)S(1)} %copy-done, f32[8,2048]{1,0:T(8,128)S(1)} %collective-permute-done.5.refs_3_, f32[16,2048]{1,0:T(8,128)S(1)} %copy-done.1, ...), custom_call_target="tpu_custom_call" | custom-call | flops 4194304 | bytes 2949636 | tf_op jit(solution)/shard_map/add_received/pallas_call | solution.py:214
  17.8 4.5 %collective-permute-start.8 = (f32[1,128]{1,0:T(1,128)S(1)}, f32[1,128]{1,0:T(1,128)S(1)}, u32[]{:S(2)}, u32[]{:S(2)}) collective-permute-start(f32[1,128]{1,0:T(1,128)S(1)} %get-tuple-element.26.refs_2_), channel_id=1, source_target_pairs={{0,3},{1,2},{2,1},{3,0},{4,7},{5,6},{6,5},{7,4},{8,11},{9,10},{10,... | collective-permute-start | bytes 1544 | tf_op jit(solution)/shard_map/ppermute | solution.py:360
  22.2 0.2 collective-permute-start.7
  22.5 0.2 collective-permute-start.6
  22.7 0.8 %collective-permute-done.8.refs_5_ = f32[1,128]{1,0:T(1,128)S(1)} collective-permute-done((f32[1,128]{1,0:T(1,128)S(1)}, f32[1,128]{1,0:T(1,128)S(1)}, u32[]{:S(2)}, u32[]{:S(2)}) %collective-permute-start.8) | collective-permute-done | bytes 544 | tf_op jit(solution)/shard_map/ppermute | solution.py:360
  23.5 1.2 %collective-permute-done.7.refs_4_ = f32[1,128]{1,0:T(1,128)S(1)} collective-permute-done((f32[1,128]{1,0:T(1,128)S(1)}, f32[1,128]{1,0:T(1,128)S(1)}, u32[]{:S(2)}, u32[]{:S(2)}) %collective-permute-start.7) | collective-permute-done | bytes 544 | tf_op jit(solution)/shard_map/ppermute | solution.py:360
  24.6 0.0 collective-permute-done.6.refs_3_
  24.6 0.0 copy-done.4
  24.6 0.9 %norm.1 = bf16[128,2048]{1,0:T(8,128)(2,1)} custom-call(f32[128,2048]{1,0:T(8,128)S(1)} %get-tuple-element.25.refs_0_, f32[1,2048]{1,0:T(1,128)S(1)} %bitcast.5, f32[1,128]{1,0:T(1,128)S(1)} %get-tuple-element.26.refs_2_, f32[1,128]{1,0:T(1,128)S(1)} %collective-permute-done.6.refs_3_, f32[1,128]{1,0:T(1,128)S(1)} %collective-permute-done.7.refs_4_, ...), custom_call_target="tpu_custom_call" | custom-call | flops 524288 | bytes 1583104 | tf_op jit(solution)/shard_map/norm/pallas_call | solution.py:214
  (7 shorter events, 0.1 us)
Async XLA Ops:
  0.0 3.3 %copy-start.1 = (f32[16,2048]{1,0:T(8,128)S(1)}, f32[16,2048]{1,0:T(8,128)}, u32[]{:S(2)}) copy-start(f32[16,2048]{1,0:T(8,128)} %refs_4_.1) | copy-start | bytes 393220
  2.0 4.0 %collective-permute-start = (f32[8,2048]{1,0:T(8,128)S(1)}, f32[8,2048]{1,0:T(8,128)S(1)}, u32[]{:S(2)}, u32[]{:S(2)}) collective-permute-start(f32[8,2048]{1,0:T(8,128)S(1)} %get-tuple-element.16), channel_id=1, source_target_pairs={{0,4},{4,0},{8,12},{12,8},{16,20},{20,16},{24,28},{28,24},{1,5},{5... | collective-permute-start | bytes 196616 | tf_op jit(solution)/shard_map/ppermute | solution.py:257
  3.3 1.0 %copy-start = (bf16[128,2048]{1,0:T(8,128)(2,1)S(1)}, bf16[128,2048]{1,0:T(8,128)(2,1)}, u32[]{:S(2)}) copy-start(bf16[128,2048]{1,0:T(8,128)(2,1)} %refs_2_.7) | copy-start | bytes 1572868
  3.3 1.1 %copy-start.2 = (f32[16,2048]{1,0:T(8,128)S(1)}, f32[16,2048]{1,0:T(8,128)}, u32[]{:S(2)}) copy-start(f32[16,2048]{1,0:T(8,128)} %refs_5_.3) | copy-start | bytes 393220
  3.3 1.1 %copy-start.3 = (f32[2048]{0:T(1024)S(1)}, f32[2048]{0:T(1024)}, u32[]{:S(2)}) copy-start(f32[2048]{0:T(1024)} %param.12) | copy-start | bytes 24580
  6.0 4.3 %collective-permute-start.1 = (f32[8,2048]{1,0:T(8,128)S(1)}, f32[8,2048]{1,0:T(8,128)S(1)}, u32[]{:S(2)}, u32[]{:S(2)}) collective-permute-start(f32[8,2048]{1,0:T(8,128)S(1)} %get-tuple-element.21), channel_id=1, source_target_pairs={{0,8},{1,9},{2,10},{3,11},{4,12},{5,13},{6,14},{7,15},{8,16},{9,17... | collective-permute-start | bytes 196616 | tf_op jit(solution)/shard_map/ppermute | solution.py:303
  6.1 4.4 %collective-permute-start.3 = (f32[8,2048]{1,0:T(8,128)S(1)}, f32[8,2048]{1,0:T(8,128)S(1)}, u32[]{:S(2)}, u32[]{:S(2)}) collective-permute-start(f32[8,2048]{1,0:T(8,128)S(1)} %get-tuple-element.21), channel_id=1, source_target_pairs={{0,1},{1,0},{2,3},{3,2},{4,5},{5,4},{6,7},{7,6},{8,9},{9,8},{10,11... | collective-permute-start | bytes 196616 | tf_op jit(solution)/shard_map/ppermute | solution.py:303
  8.4 4.0 %collective-permute-start.2 = (f32[8,2048]{1,0:T(8,128)S(1)}, f32[8,2048]{1,0:T(8,128)S(1)}, u32[]{:S(2)}, u32[]{:S(2)}) collective-permute-start(f32[8,2048]{1,0:T(8,128)S(1)} %get-tuple-element.21), channel_id=1, source_target_pairs={{0,16},{1,17},{2,18},{3,19},{4,20},{5,21},{6,22},{7,23},{8,9},{9,8... | collective-permute-start | bytes 196616 | tf_op jit(solution)/shard_map/ppermute | solution.py:303
  10.4 3.2 %collective-permute-start.4 = (f32[8,2048]{1,0:T(8,128)S(1)}, f32[8,2048]{1,0:T(8,128)S(1)}, u32[]{:S(2)}, u32[]{:S(2)}) collective-permute-start(f32[8,2048]{1,0:T(8,128)S(1)} %add_select_fusion), channel_id=1, source_target_pairs={{0,1},{1,0},{2,3},{3,2},{4,5},{5,4},{6,7},{7,6},{8,24},{9,25},{10,... | collective-permute-start | bytes 196616 | tf_op jit(solution)/shard_map/ppermute | solution.py:303
  13.6 3.2 %collective-permute-start.5 = (f32[8,2048]{1,0:T(8,128)S(1)}, f32[8,2048]{1,0:T(8,128)S(1)}, u32[]{:S(2)}, u32[]{:S(2)}) collective-permute-start(f32[8,2048]{1,0:T(8,128)S(1)} %get-tuple-element.27), channel_id=1, source_target_pairs={{0,4},{4,0},{8,12},{12,8},{16,20},{20,16},{24,28},{28,24},{1,5},{5... | collective-permute-start | bytes 196616 | tf_op jit(solution)/shard_map/ppermute | solution.py:336
  16.8 7.9 %copy-start.4 = (f32[2048]{0:T(1024)S(1)}, f32[2048]{0:T(1024)}, u32[]{:S(2)}) copy-start(f32[2048]{0:T(1024)} %param.13) | copy-start | bytes 24580
  17.8 5.7 %collective-permute-start.8 = (f32[1,128]{1,0:T(1,128)S(1)}, f32[1,128]{1,0:T(1,128)S(1)}, u32[]{:S(2)}, u32[]{:S(2)}) collective-permute-start(f32[1,128]{1,0:T(1,128)S(1)} %get-tuple-element.26.refs_2_), channel_id=1, source_target_pairs={{0,3},{1,2},{2,1},{3,0},{4,7},{5,6},{6,5},{7,4},{8,11},{9,10},{10,... | collective-permute-start | bytes 1544 | tf_op jit(solution)/shard_map/ppermute | solution.py:360
  22.2 2.4 %collective-permute-start.7 = (f32[1,128]{1,0:T(1,128)S(1)}, f32[1,128]{1,0:T(1,128)S(1)}, u32[]{:S(2)}, u32[]{:S(2)}) collective-permute-start(f32[1,128]{1,0:T(1,128)S(1)} %get-tuple-element.26.refs_2_), channel_id=1, source_target_pairs={{0,2},{1,3},{2,0},{3,1},{4,6},{5,7},{6,4},{7,5},{8,10},{9,11},{10,... | collective-permute-start | bytes 1544 | tf_op jit(solution)/shard_map/ppermute | solution.py:360
  22.5 2.2 %collective-permute-start.6 = (f32[1,128]{1,0:T(1,128)S(1)}, f32[1,128]{1,0:T(1,128)S(1)}, u32[]{:S(2)}, u32[]{:S(2)}) collective-permute-start(f32[1,128]{1,0:T(1,128)S(1)} %get-tuple-element.26.refs_2_), channel_id=1, source_target_pairs={{0,1},{1,0},{2,3},{3,2},{4,5},{5,4},{6,7},{7,6},{8,9},{9,8},{10,11... | collective-permute-start | bytes 1544 | tf_op jit(solution)/shard_map/ppermute | solution.py:360

commit v5 on v4

--- a/solution.py
+++ b/solution.py
@@ -21,7 +21,8 @@
 def added(terms):
     terms = list(terms)
     while len(terms) > 1:
-        terms = [a + b for a, b in zip(terms[::2], terms[1::2])]
+        odd = terms[len(terms) - len(terms) % 2:]
+        terms = [a + b for a, b in zip(terms[::2], terms[1::2])] + odd
     return terms[0]
 
 
@@ -356,8 +357,11 @@
         name="add_received",
     )
 
+    def across(i, by):
+        return i ^ by if tp & (tp - 1) == 0 else (i + by) % tp
+
     parts = [squares] + [
-        lax.ppermute(squares, "tp", [(i, i ^ by) for i in range(tp)]) for by in (1, 2, 3)
+        lax.ppermute(squares, "tp", [(i, across(i, by)) for i in range(tp)]) for by in range(1, tp)
     ]
     (out,) = call(
         lambda *refs: norm_kernel(len(parts), *refs),

time: 25.7 us -> 25.7 us (level)
  no operation moved by 1% of the time
where the time goes in v5:
time: 25.7 us; the launch traced here: 25.6 us
  starting transfers between devices  10.4 us (40%)
  Pallas kernels  8.75 us (34%)
  waiting for transfers between devices  5.97 us (23%)
    pallas_call x7, Pallas kernels, call(): pl.pallas_call(kernel, out_shape=outputs, in_specs=specs, out_specs=out_s...  8.75 us
    ppermute x3, starting transfers between devices, body(): lax.ppermute(squares, 'tp', [(i, across(i, by)) for i in range(tp)])  4.96 us
    ppermute x4, waiting for transfers between devices, moved(): return lax.ppermute(array, ('ctx', 'tp'), links)  3.01 us
    ppermute x4, starting transfers between devices, moved(): return lax.ppermute(array, ('ctx', 'tp'), links)  2.88 us
    ppermute x3, waiting for transfers between devices, body(): lax.ppermute(squares, 'tp', [(i, across(i, by)) for i in range(tp)])  1.92 us
    ppermute x1, starting transfers between devices, body(): partner = lax.ppermute(other, 'ctx', pair)  1.28 us
    ppermute x1, starting transfers between devices, body(): received = lax.ppermute(jnp.where(x == 0, second, before), 'ctx', pair)  1.28 us
    ppermute x1, waiting for transfers between devices, body(): received = lax.ppermute(jnp.where(x == 0, second, before), 'ctx', pair)  1.04 us
  transfers between devices with their start and end apart: 9, of which 5 were waited for; matrix products, arithmetic and copies ran while one was open for 0% of the time, Pallas kernels for 19%

profile of v5, /device:TPU:17, one launch (start us, length us, event | category | flops | bytes accessed | tf_op | source)
XLA Modules:
  0.0 25.6 jit_solution(13940805926447851847)
XLA Ops:
  0.0 2.0 %first_ends.1 = (f32[8,2048]{1,0:T(8,128)S(1)}, f32[128,2048]{1,0:T(8,128)S(1)}) custom-call(s32[1]{0:T(128)} %bitcast.refs_0_.x_ref, bf16[128,2048]{1,0:T(8,128)(2,1)} %refs_1_.1, bf16[128,2048]{1,0:T(8,128)(2,1)} %refs_2_.4, f32[16,2048]{1,0:T(8,128)} %refs_4_.1), custom_call_target="tpu_custom_call" | custom-call | flops 4194304 | bytes 2293764 | tf_op jit(solution)/shard_map/first_ends/pallas_call | solution.py:215
  2.0 1.3 %collective-permute-start = (f32[8,2048]{1,0:T(8,128)S(1)}, f32[8,2048]{1,0:T(8,128)S(1)}, u32[]{:S(2)}, u32[]{:S(2)}) collective-permute-start(f32[8,2048]{1,0:T(8,128)S(1)} %get-tuple-element.16), channel_id=1, source_target_pairs={{0,4},{4,0},{8,12},{12,8},{16,20},{20,16},{24,28},{28,24},{1,5},{5... | collective-permute-start | bytes 196616 | tf_op jit(solution)/shard_map/ppermute | solution.py:258
  3.2 0.0 copy-done.1
  3.3 0.0 copy-start
  3.3 0.0 copy-start.2
  3.3 0.8 %second_ends.1 = f32[8,2048]{1,0:T(8,128)S(1)} custom-call(s32[1]{0:T(128)} %bitcast.refs_0_.x_ref, f32[128,2048]{1,0:T(8,128)S(1)} %get-tuple-element.22.driven.refs_1_, f32[16,2048]{1,0:T(8,128)S(1)} %copy-done.1), custom_call_target="tpu_custom_call" | custom-call | flops 4194304 | bytes 1245188 | tf_op jit(solution)/shard_map/second_ends/pallas_call | solution.py:215
  4.1 0.2 copy-done
  4.3 0.0 copy-done.2
  4.3 0.0 copy-done.3
  4.3 1.6 %local_filter.2.refs_1_ = f32[128,1024]{1,0:T(8,128)S(1)} custom-call(bf16[128,2048]{1,0:T(8,128)(2,1)S(1)} %copy-done, f32[128,2048]{1,0:T(8,128)S(1)} %get-tuple-element.22.driven.refs_1_, f32[16,2048]{1,0:T(8,128)S(1)} %copy-done.1, f32[16,2048]{1,0:T(8,128)S(1)} %copy-done.2, f32[1,2048]{1,0:T(1,128)S(1)} %bitcast.3), custom_call_target="tpu_custom_call" | custom-call | flops 8388608 | bytes 2367488 | tf_op jit(solution)/shard_map/local_filter/pallas_call | solution.py:215
  5.9 0.0 collective-permute-done
  6.0 0.1 collective-permute-start.1
  6.1 2.3 %collective-permute-start.3 = (f32[8,2048]{1,0:T(8,128)S(1)}, f32[8,2048]{1,0:T(8,128)S(1)}, u32[]{:S(2)}, u32[]{:S(2)}) collective-permute-start(f32[8,2048]{1,0:T(8,128)S(1)} %get-tuple-element.21), channel_id=1, source_target_pairs={{0,1},{1,0},{2,3},{3,2},{4,5},{5,4},{6,7},{7,6},{8,9},{9,8},{10,11... | collective-permute-start | bytes 196616 | tf_op jit(solution)/shard_map/ppermute | solution.py:304
  8.4 0.3 %collective-permute-start.2 = (f32[8,2048]{1,0:T(8,128)S(1)}, f32[8,2048]{1,0:T(8,128)S(1)}, u32[]{:S(2)}, u32[]{:S(2)}) collective-permute-start(f32[8,2048]{1,0:T(8,128)S(1)} %get-tuple-element.21), channel_id=1, source_target_pairs={{0,16},{1,17},{2,18},{3,19},{4,20},{5,21},{6,22},{7,23},{8,9},{9,8... | collective-permute-start | bytes 196616 | tf_op jit(solution)/shard_map/ppermute | solution.py:304
  8.7 1.6 %local_filter.3.refs_2_ = f32[128,1024]{1,0:T(8,128)S(1)} custom-call(bf16[128,2048]{1,0:T(8,128)(2,1)S(1)} %copy-done, f32[128,2048]{1,0:T(8,128)S(1)} %get-tuple-element.22.driven.refs_1_, f32[16,2048]{1,0:T(8,128)S(1)} %copy-done.1, f32[16,2048]{1,0:T(8,128)S(1)} %copy-done.2, f32[1,2048]{1,0:T(1,128)S(1)} %bitcast.4), custom_call_target="tpu_custom_call" | custom-call | flops 8388608 | bytes 2367488 | tf_op jit(solution)/shard_map/local_filter/pallas_call | solution.py:215
  10.3 0.0 collective-permute-done.1
  10.4 0.2 collective-permute-start.4
  10.5 0.0 collective-permute-done.3
  10.5 1.9 %collective-permute-done.2 = f32[8,2048]{1,0:T(8,128)S(1)} collective-permute-done((f32[8,2048]{1,0:T(8,128)S(1)}, f32[8,2048]{1,0:T(8,128)S(1)}, u32[]{:S(2)}, u32[]{:S(2)}) %collective-permute-start.2) | collective-permute-done | bytes 65568 | tf_op jit(solution)/shard_map/ppermute | solution.py:304
  12.4 1.1 %collective-permute-done.4 = f32[8,2048]{1,0:T(8,128)S(1)} collective-permute-done((f32[8,2048]{1,0:T(8,128)S(1)}, f32[8,2048]{1,0:T(8,128)S(1)}, u32[]{:S(2)}, u32[]{:S(2)}) %collective-permute-start.4) | collective-permute-done | bytes 65568 | tf_op jit(solution)/shard_map/ppermute | solution.py:304
  13.6 1.3 %collective-permute-start.5 = (f32[8,2048]{1,0:T(8,128)S(1)}, f32[8,2048]{1,0:T(8,128)S(1)}, u32[]{:S(2)}, u32[]{:S(2)}) collective-permute-start(f32[8,2048]{1,0:T(8,128)S(1)} %get-tuple-element.27), channel_id=1, source_target_pairs={{0,4},{4,0},{8,12},{12,8},{16,20},{20,16},{24,28},{28,24},{1,5},{5... | collective-permute-start | bytes 196616 | tf_op jit(solution)/shard_map/ppermute | solution.py:337
  14.9 0.8 %add_kept.1.refs_1_ = f32[128,2048]{1,0:T(8,128)S(1)} custom-call(s32[1]{0:T(128)} %bitcast.refs_0_.x_ref, f32[128,1024]{1,0:T(8,128)S(1)} %local_filter.2.refs_1_, f32[128,1024]{1,0:T(8,128)S(1)} %local_filter.3.refs_2_, bf16[128,2048]{1,0:T(8,128)(2,1)S(1)} %copy-done, f32[8,2048]{1,0:T(8,128)S(1)} %broadcast_select_fusion.1.refs_4_, ...), custom_call_target="tpu_custom_call" | custom-call | flops 4194304 | bytes 2949124 | tf_op jit(solution)/shard_map/add_kept/pallas_call | solution.py:215
  15.7 1.0 %collective-permute-done.5.refs_3_ = f32[8,2048]{1,0:T(8,128)S(1)} collective-permute-done((f32[8,2048]{1,0:T(8,128)S(1)}, f32[8,2048]{1,0:T(8,128)S(1)}, u32[]{:S(2)}, u32[]{:S(2)}) %collective-permute-start.5) | collective-permute-done | bytes 65568 | tf_op jit(solution)/shard_map/ppermute | solution.py:337
  16.8 1.0 %add_received.1 = (f32[128,2048]{1,0:T(8,128)S(1)}, f32[1,128]{1,0:T(1,128)S(1)}) custom-call(s32[1]{0:T(128)} %bitcast.refs_0_.x_ref, f32[128,2048]{1,0:T(8,128)S(1)} %add_kept.1.refs_1_, bf16[128,2048]{1,0:T(8,128)(2,1)S(1)} %copy-done, f32[8,2048]{1,0:T(8,128)S(1)} %collective-permute-done.5.refs_3_, f32[16,2048]{1,0:T(8,128)S(1)} %copy-done.1, ...), custom_call_target="tpu_custom_call" | custom-call | flops 4194304 | bytes 2949636 | tf_op jit(solution)/shard_map/add_received/pallas_call | solution.py:215
  17.8 4.5 %collective-permute-start.8 = (f32[1,128]{1,0:T(1,128)S(1)}, f32[1,128]{1,0:T(1,128)S(1)}, u32[]{:S(2)}, u32[]{:S(2)}) collective-permute-start(f32[1,128]{1,0:T(1,128)S(1)} %get-tuple-element.26.refs_2_), channel_id=1, source_target_pairs={{0,3},{1,2},{2,1},{3,0},{4,7},{5,6},{6,5},{7,4},{8,11},{9,10},{10,... | collective-permute-start | bytes 1544 | tf_op jit(solution)/shard_map/ppermute | solution.py:364
  22.2 0.2 collective-permute-start.7
  22.5 0.2 collective-permute-start.6
  22.7 0.8 %collective-permute-done.8.refs_5_ = f32[1,128]{1,0:T(1,128)S(1)} collective-permute-done((f32[1,128]{1,0:T(1,128)S(1)}, f32[1,128]{1,0:T(1,128)S(1)}, u32[]{:S(2)}, u32[]{:S(2)}) %collective-permute-start.8) | collective-permute-done | bytes 544 | tf_op jit(solution)/shard_map/ppermute | solution.py:364
  23.5 1.2 %collective-permute-done.7.refs_4_ = f32[1,128]{1,0:T(1,128)S(1)} collective-permute-done((f32[1,128]{1,0:T(1,128)S(1)}, f32[1,128]{1,0:T(1,128)S(1)}, u32[]{:S(2)}, u32[]{:S(2)}) %collective-permute-start.7) | collective-permute-done | bytes 544 | tf_op jit(solution)/shard_map/ppermute | solution.py:364
  24.6 0.0 collective-permute-done.6.refs_3_
  24.6 0.0 copy-done.4
  24.6 0.9 %norm.1 = bf16[128,2048]{1,0:T(8,128)(2,1)} custom-call(f32[128,2048]{1,0:T(8,128)S(1)} %get-tuple-element.25.refs_0_, f32[1,2048]{1,0:T(1,128)S(1)} %bitcast.5, f32[1,128]{1,0:T(1,128)S(1)} %get-tuple-element.26.refs_2_, f32[1,128]{1,0:T(1,128)S(1)} %collective-permute-done.6.refs_3_, f32[1,128]{1,0:T(1,128)S(1)} %collective-permute-done.7.refs_4_, ...), custom_call_target="tpu_custom_call" | custom-call | flops 524288 | bytes 1583104 | tf_op jit(solution)/shard_map/norm/pallas_call | solution.py:215
  (7 shorter events, 0.1 us)
Async XLA Ops:
  0.0 3.3 %copy-start.1 = (f32[16,2048]{1,0:T(8,128)S(1)}, f32[16,2048]{1,0:T(8,128)}, u32[]{:S(2)}) copy-start(f32[16,2048]{1,0:T(8,128)} %refs_4_.1) | copy-start | bytes 393220
  2.0 4.0 %collective-permute-start = (f32[8,2048]{1,0:T(8,128)S(1)}, f32[8,2048]{1,0:T(8,128)S(1)}, u32[]{:S(2)}, u32[]{:S(2)}) collective-permute-start(f32[8,2048]{1,0:T(8,128)S(1)} %get-tuple-element.16), channel_id=1, source_target_pairs={{0,4},{4,0},{8,12},{12,8},{16,20},{20,16},{24,28},{28,24},{1,5},{5... | collective-permute-start | bytes 196616 | tf_op jit(solution)/shard_map/ppermute | solution.py:258
  3.3 1.0 %copy-start = (bf16[128,2048]{1,0:T(8,128)(2,1)S(1)}, bf16[128,2048]{1,0:T(8,128)(2,1)}, u32[]{:S(2)}) copy-start(bf16[128,2048]{1,0:T(8,128)(2,1)} %refs_2_.7) | copy-start | bytes 1572868
  3.3 1.1 %copy-start.2 = (f32[16,2048]{1,0:T(8,128)S(1)}, f32[16,2048]{1,0:T(8,128)}, u32[]{:S(2)}) copy-start(f32[16,2048]{1,0:T(8,128)} %refs_5_.3) | copy-start | bytes 393220
  3.3 1.1 %copy-start.3 = (f32[2048]{0:T(1024)S(1)}, f32[2048]{0:T(1024)}, u32[]{:S(2)}) copy-start(f32[2048]{0:T(1024)} %param.12) | copy-start | bytes 24580
  6.0 4.3 %collective-permute-start.1 = (f32[8,2048]{1,0:T(8,128)S(1)}, f32[8,2048]{1,0:T(8,128)S(1)}, u32[]{:S(2)}, u32[]{:S(2)}) collective-permute-start(f32[8,2048]{1,0:T(8,128)S(1)} %get-tuple-element.21), channel_id=1, source_target_pairs={{0,8},{1,9},{2,10},{3,11},{4,12},{5,13},{6,14},{7,15},{8,16},{9,17... | collective-permute-start | bytes 196616 | tf_op jit(solution)/shard_map/ppermute | solution.py:304
  6.1 4.4 %collective-permute-start.3 = (f32[8,2048]{1,0:T(8,128)S(1)}, f32[8,2048]{1,0:T(8,128)S(1)}, u32[]{:S(2)}, u32[]{:S(2)}) collective-permute-start(f32[8,2048]{1,0:T(8,128)S(1)} %get-tuple-element.21), channel_id=1, source_target_pairs={{0,1},{1,0},{2,3},{3,2},{4,5},{5,4},{6,7},{7,6},{8,9},{9,8},{10,11... | collective-permute-start | bytes 196616 | tf_op jit(solution)/shard_map/ppermute | solution.py:304
  8.4 4.0 %collective-permute-start.2 = (f32[8,2048]{1,0:T(8,128)S(1)}, f32[8,2048]{1,0:T(8,128)S(1)}, u32[]{:S(2)}, u32[]{:S(2)}) collective-permute-start(f32[8,2048]{1,0:T(8,128)S(1)} %get-tuple-element.21), channel_id=1, source_target_pairs={{0,16},{1,17},{2,18},{3,19},{4,20},{5,21},{6,22},{7,23},{8,9},{9,8... | collective-permute-start | bytes 196616 | tf_op jit(solution)/shard_map/ppermute | solution.py:304
  10.4 3.2 %collective-permute-start.4 = (f32[8,2048]{1,0:T(8,128)S(1)}, f32[8,2048]{1,0:T(8,128)S(1)}, u32[]{:S(2)}, u32[]{:S(2)}) collective-permute-start(f32[8,2048]{1,0:T(8,128)S(1)} %add_select_fusion), channel_id=1, source_target_pairs={{0,1},{1,0},{2,3},{3,2},{4,5},{5,4},{6,7},{7,6},{8,24},{9,25},{10,... | collective-permute-start | bytes 196616 | tf_op jit(solution)/shard_map/ppermute | solution.py:304
  13.6 3.2 %collective-permute-start.5 = (f32[8,2048]{1,0:T(8,128)S(1)}, f32[8,2048]{1,0:T(8,128)S(1)}, u32[]{:S(2)}, u32[]{:S(2)}) collective-permute-start(f32[8,2048]{1,0:T(8,128)S(1)} %get-tuple-element.27), channel_id=1, source_target_pairs={{0,4},{4,0},{8,12},{12,8},{16,20},{20,16},{24,28},{28,24},{1,5},{5... | collective-permute-start | bytes 196616 | tf_op jit(solution)/shard_map/ppermute | solution.py:337
  16.8 7.9 %copy-start.4 = (f32[2048]{0:T(1024)S(1)}, f32[2048]{0:T(1024)}, u32[]{:S(2)}) copy-start(f32[2048]{0:T(1024)} %param.13) | copy-start | bytes 24580
  17.8 5.7 %collective-permute-start.8 = (f32[1,128]{1,0:T(1,128)S(1)}, f32[1,128]{1,0:T(1,128)S(1)}, u32[]{:S(2)}, u32[]{:S(2)}) collective-permute-start(f32[1,128]{1,0:T(1,128)S(1)} %get-tuple-element.26.refs_2_), channel_id=1, source_target_pairs={{0,3},{1,2},{2,1},{3,0},{4,7},{5,6},{6,5},{7,4},{8,11},{9,10},{10,... | collective-permute-start | bytes 1544 | tf_op jit(solution)/shard_map/ppermute | solution.py:364
  22.2 2.4 %collective-permute-start.7 = (f32[1,128]{1,0:T(1,128)S(1)}, f32[1,128]{1,0:T(1,128)S(1)}, u32[]{:S(2)}, u32[]{:S(2)}) collective-permute-start(f32[1,128]{1,0:T(1,128)S(1)} %get-tuple-element.26.refs_2_), channel_id=1, source_target_pairs={{0,2},{1,3},{2,0},{3,1},{4,6},{5,7},{6,4},{7,5},{8,10},{9,11},{10,... | collective-permute-start | bytes 1544 | tf_op jit(solution)/shard_map/ppermute | solution.py:364
  22.5 2.2 %collective-permute-start.6 = (f32[1,128]{1,0:T(1,128)S(1)}, f32[1,128]{1,0:T(1,128)S(1)}, u32[]{:S(2)}, u32[]{:S(2)}) collective-permute-start(f32[1,128]{1,0:T(1,128)S(1)} %get-tuple-element.26.refs_2_), channel_id=1, source_target_pairs={{0,1},{1,0},{2,3},{3,2},{4,5},{5,4},{6,7},{7,6},{8,9},{9,8},{10,11... | collective-permute-start | bytes 1544 | tf_op jit(solution)/shard_map/ppermute | solution.py:364

commit v6 on v5

--- a/solution.py
+++ b/solution.py
@@ -142,7 +142,7 @@
 
 
 def carry_kernel(which, pieces, final, x_ref, *refs):
-    locals_, (query, carried, rates, residues), rest = refs[:pieces], refs[pieces:pieces + 4], refs[pieces + 4:]
+    locals_, (query, carried, rates, scales, decays8), rest = refs[:pieces], refs[pieces:pieces + 5], refs[pieces + 5:]
     if final:
         gated, squares, decay, decay8, weights, turn, sums = rest
         sums[...] = jnp.zeros_like(sums)
@@ -155,8 +155,8 @@
     rate = rates[rows, :]
     step = jnp.exp(-rate)
     decay[...] = step
-    decay8[...] = jnp.exp(-ROWS * rate)
-    weights[...] = residues[rows, :] * jnp.sqrt(1.0 - step * step) * carried[...]
+    decay8[...] = decays8[rows, :]
+    weights[...] = scales[rows, :] * carried[...]
     groups = width // LANES // pieces
 
     for piece, local in enumerate(locals_):
@@ -185,6 +185,15 @@
         squares[...] = jnp.sum(jnp.transpose(sums[...]), axis=0, keepdims=True)
 
 
+def scale_kernel(rates, residues, scales):
+    decay = jnp.exp(-rates[...])
+    scales[...] = residues[...] * jnp.sqrt(1.0 - decay * decay)
+
+
+def decay_kernel(rates, decay8):
+    decay8[...] = jnp.exp(-ROWS * rates[...])
+
+
 def norm_kernel(parts, gated, gain, *rest):
     sums, (out, factors, buf, sems) = rest[:parts], rest[parts:]
     count, width = gated.shape
@@ -291,6 +300,9 @@
     pair_state = jnp.where(x == 0, mine * step + partner, partner * step + mine)
     pair_state, driven = tied((pair_state, driven))
 
+    def to_partner(before):
+        return jnp.where(x == 0, before * step + mine, before)
+
     def late_parts():
         return [local_part(part, driven) for part in range(pieces // 2, pieces)]
 
@@ -303,24 +315,38 @@
             links = [(i * tp + j, target(i, j)) for i in range(ctx) for j in range(tp)]
             return lax.ppermute(array, ("ctx", "tp"), links)
 
+        def traded(array, pairs):
+            links = []
+            for i in range(ctx):
+                for j in range(tp):
+                    links.append((i * tp + j, (i ^ 1) * tp + j if i // 2 in pairs else i * tp + (j ^ 1)))
+            return lax.ppermute(array, ("ctx", "tp"), links)
+
         span = jnp.exp(-my_rates * (2 * count))
-        first_move = moved(pair_state, (1, 2, 0, 3))
-        second_move = moved(pair_state, (0, 1, 3, 2))
-        third_move = moved(pair_state, (2, 1, 0, 3))
-        late = late_parts()
-        first_move, late = tied((first_move, late))
+        pair_state, rates = tied((pair_state, rates))
+        first_move = moved(pair_state, (1, 0, 2, 3))
+        second_move = moved(pair_state, (2, 0, 3, 1))
+        third_move = moved(pair_state, (0, 2, 1, 3))
+        (scales,) = call(scale_kernel, (rates, residues), [VMEM] * 2, (f32(modes, width),), name="scales")
+        first_move, scales = tied((first_move, scales))
         both = jnp.where(z == 1, span * first_move + pair_state, pair_state)
         handed = moved(both, (0, 3, 1, 2))
+        sooner = to_partner(jnp.where(z == 1, first_move, 0.0))
+        sooner, rates = tied((sooner, rates))
+        got = traded(sooner, (0, 1))
+        (decays8,) = call(decay_kernel, (rates,), [VMEM], (f32(modes, width),), flops=10**9, name="decays")
+        handed, decays8 = tied((handed, decays8))
         before = jnp.where(
             z == 0,
             0.0,
-            jnp.where(z == 1, first_move, jnp.where(z == 2, first_move + span * third_move, second_move + span * handed)),
+            jnp.where(z == 1, first_move, jnp.where(z == 2, third_move + span * second_move, second_move + span * handed)),
         )
+        received = jnp.where(z <= 1, got, traded(to_partner(before), (2, 3)))
     else:
         span = min(3, outer - 1)
         parts = [shifted(pair_state, by) for by in range(span, 0, -1)]
-        late = late_parts()
-        parts, late = tied((parts, late))
+        (scales,) = call(scale_kernel, (rates, residues), [VMEM] * 2, (f32(modes, width),), name="scales")
+        (decays8,) = call(decay_kernel, (rates,), [VMEM], (f32(modes, width),), flops=10**9, name="decays")
         before = jnp.zeros_like(mine)
         for by, states in zip(range(span, 0, -1), parts):
             weight = jnp.exp(-my_rates * (2 * count * (by - 1)))
@@ -331,17 +357,18 @@
                 weight = jnp.exp(-my_rates * (2 * count * by))
                 before = before + jnp.where(z >= by, weight * states, 0.0)
             span = 4 * span
-
-    second = before * step + jnp.where(x == 0, mine, partner)
-    kept = jnp.where(x == 0, before, second)
-    received = lax.ppermute(jnp.where(x == 0, second, before), "ctx", pair)
+        received = lax.ppermute(to_partner(before), "ctx", pair)
+
+    before, driven = tied((before, driven))
+    late = late_parts()
+    kept = jnp.where(x == 0, before, before * step + partner)
 
     carry_scratch = [*[vmem(half, width)] * 3, vmem(2, half * ROWS, LANES)]
     locals_ = early + late
     (halfway,) = call(
         lambda *refs: carry_kernel(0, pieces, False, *refs),
-        (x_ref, *locals_, query, kept, rates, residues),
-        [SMEM] + [VMEM] * (pieces + 4),
+        (x_ref, *locals_, query, kept, rates, scales, decays8),
+        [SMEM] + [VMEM] * (pieces + 5),
         (f32(count, width),),
         scratch=carry_scratch,
         flops=work,
@@ -349,20 +376,24 @@
     )
     gated, squares = call(
         lambda *refs: carry_kernel(1, 1, True, *refs),
-        (x_ref, halfway, query, received, rates, residues),
-        [SMEM] + [VMEM] * 5,
+        (x_ref, halfway, query, received, rates, scales, decays8),
+        [SMEM] + [VMEM] * 6,
         (f32(count, width), f32(1, count)),
         scratch=[*carry_scratch, vmem(count, LANES)],
         flops=work,
         name="add_received",
     )
 
-    def across(i, by):
-        return i ^ by if tp & (tp - 1) == 0 else (i + by) % tp
-
-    parts = [squares] + [
-        lax.ppermute(squares, "tp", [(i, across(i, by)) for i in range(tp)]) for by in range(1, tp)
-    ]
+    parts = [squares]
+    if tp & (tp - 1) == 0:
+        mask = 1
+        while mask < tp:
+            parts = [added(parts)]
+            parts.append(lax.ppermute(parts[0], "tp", [(i, i ^ mask) for i in range(tp)]))
+            mask = 2 * mask + 1
+    else:
+        for by in range(1, tp):
+            parts.append(lax.ppermute(squares, "tp", [(i, (i + by) % tp) for i in range(tp)]))
     (out,) = call(
         lambda *refs: norm_kernel(len(parts), *refs),
         (gated, gain[None], *parts),

time: 25.7 us -> 24.8 us (0.965)
  the two profiles are of different devices: /device:TPU:17 before, /device:TPU:31 now
where the time goes in v6:
time: 24.8 us; the launch traced here: 24.6 us
  Pallas kernels  8.8 us (35%)
  starting transfers between devices  8.14 us (33%)
  waiting for transfers between devices  7.18 us (29%)
  local copies, waits for them, and re-layouts  0.25 us (1%)
    pallas_call x9, Pallas kernels, call(): pl.pallas_call(kernel, out_shape=outputs, in_specs=specs, out_specs=out_s...  8.8 us
    ppermute x4, starting transfers between devices, moved(): return lax.ppermute(array, ('ctx', 'tp'), links)  3.51 us
    ppermute x2, waiting for transfers between devices, body(): lax.ppermute(parts[0], 'tp', [(i, i ^ mask) for i in range(tp)])  3.37 us
    ppermute x4, waiting for transfers between devices, moved(): return lax.ppermute(array, ('ctx', 'tp'), links)  3.23 us
    ppermute x2, starting transfers between devices, body(): lax.ppermute(parts[0], 'tp', [(i, i ^ mask) for i in range(tp)])  3.02 us
    ppermute x2, starting transfers between devices, traded(): return lax.ppermute(array, ('ctx', 'tp'), links)  1.29 us
  transfers between devices with their start and end apart: 9, of which 5 were waited for; matrix products, arithmetic and copies ran while one was open for 0% of the time, Pallas kernels for 20%

profile of v6, /device:TPU:31, one launch (start us, length us, event | category | flops | bytes accessed | tf_op | source)
XLA Modules:
  0.0 24.6 jit_solution(6010155401157640672)
XLA Ops:
  0.0 2.0 %first_ends.1 = (f32[8,2048]{1,0:T(8,128)S(1)}, f32[128,2048]{1,0:T(8,128)S(1)}) custom-call(s32[1]{0:T(128)} %bitcast.refs_0_.x_ref, bf16[128,2048]{1,0:T(8,128)(2,1)} %refs_1_.1, bf16[128,2048]{1,0:T(8,128)(2,1)} %refs_2_.3, f32[16,2048]{1,0:T(8,128)} %refs_4_), custom_call_target="tpu_custom_call" | custom-call | flops 4194304 | bytes 2293764 | tf_op jit(solution)/shard_map/first_ends/pallas_call | solution.py:224
  2.0 0.3 %collective-permute-start = (f32[8,2048]{1,0:T(8,128)S(1)}, f32[8,2048]{1,0:T(8,128)S(1)}, u32[]{:S(2)}, u32[]{:S(2)}) collective-permute-start(f32[8,2048]{1,0:T(8,128)S(1)} %get-tuple-element.24), channel_id=1, source_target_pairs={{0,4},{4,0},{8,12},{12,8},{16,20},{20,16},{24,28},{28,24},{1,5},{5... | collective-permute-start | bytes 196616 | tf_op jit(solution)/shard_map/ppermute | solution.py:267
  2.3 0.0 copy-done
  2.3 0.8 %second_ends.1 = f32[8,2048]{1,0:T(8,128)S(1)} custom-call(s32[1]{0:T(128)} %bitcast.refs_0_.x_ref, f32[128,2048]{1,0:T(8,128)S(1)} %get-tuple-element.36.driven.refs_1_, f32[16,2048]{1,0:T(8,128)S(1)} %copy-done), custom_call_target="tpu_custom_call" | custom-call | flops 4194304 | bytes 1245188 | tf_op jit(solution)/shard_map/second_ends/pallas_call | solution.py:224
  3.1 0.2 copy-done.1
  3.3 0.0 copy-done.2
  3.4 0.0 copy-done.3
  3.4 1.6 %local_filter.2.refs_1_ = f32[128,1024]{1,0:T(8,128)S(1)} custom-call(bf16[128,2048]{1,0:T(8,128)(2,1)S(1)} %copy-done.1, f32[128,2048]{1,0:T(8,128)S(1)} %get-tuple-element.36.driven.refs_1_, f32[16,2048]{1,0:T(8,128)S(1)} %copy-done, f32[16,2048]{1,0:T(8,128)S(1)} %copy-done.2, f32[1,2048]{1,0:T(1,128)S(1)} %bitcast.3), custom_call_target="tpu_custom_call" | custom-call | flops 8388608 | bytes 2367488 | tf_op jit(solution)/shard_map/local_filter/pallas_call | solution.py:224
  5.0 0.2 collective-permute-done
  5.2 1.9 %collective-permute-start.1 = (f32[8,2048]{1,0:T(8,128)S(1)}, f32[8,2048]{1,0:T(8,128)S(1)}, u32[]{:S(2)}, u32[]{:S(2)}) collective-permute-start(f32[8,2048]{1,0:T(8,128)S(1)} %get-tuple-element.30), channel_id=1, source_target_pairs={{0,8},{1,9},{2,10},{3,11},{4,12},{5,13},{6,14},{7,15},{8,0},{9,1},... | collective-permute-start | bytes 196616 | tf_op jit(solution)/shard_map/ppermute | solution.py:316
  7.1 0.1 collective-permute-start.2
  7.2 1.3 %collective-permute-start.3 = (f32[8,2048]{1,0:T(8,128)S(1)}, f32[8,2048]{1,0:T(8,128)S(1)}, u32[]{:S(2)}, u32[]{:S(2)}) collective-permute-start(f32[8,2048]{1,0:T(8,128)S(1)} %get-tuple-element.30), channel_id=1, source_target_pairs={{0,16},{1,17},{2,18},{3,19},{4,20},{5,21},{6,22},{7,23},{8,0},{9,1... | collective-permute-start | bytes 196616 | tf_op jit(solution)/shard_map/ppermute | solution.py:316
  8.5 0.1 scales.1.refs_6_.refs_5_
  8.5 0.0 collective-permute-done.1
  8.6 0.2 %collective-permute-start.4 = (f32[8,2048]{1,0:T(8,128)S(1)}, f32[8,2048]{1,0:T(8,128)S(1)}, u32[]{:S(2)}, u32[]{:S(2)}) collective-permute-start(f32[8,2048]{1,0:T(8,128)S(1)} %get-tuple-element.48), channel_id=1, source_target_pairs={{0,1},{1,0},{2,3},{3,2},{4,5},{5,4},{6,7},{7,6},{8,24},{9,25},{10,... | collective-permute-start | bytes 196616 | tf_op jit(solution)/shard_map/ppermute | solution.py:316
  8.8 1.0 %collective-permute-start.5 = (f32[8,2048]{1,0:T(8,128)S(1)}, f32[8,2048]{1,0:T(8,128)S(1)}, u32[]{:S(2)}, u32[]{:S(2)}) collective-permute-start(f32[8,2048]{1,0:T(8,128)S(1)} %get-tuple-element.40), channel_id=1, source_target_pairs={{0,4},{1,5},{2,6},{3,7},{4,0},{5,1},{6,2},{7,3},{8,12},{9,13},{10,... | collective-permute-start | bytes 196616 | tf_op jit(solution)/shard_map/ppermute | solution.py:323
  9.8 3.2 %collective-permute-done.4 = f32[8,2048]{1,0:T(8,128)S(1)} collective-permute-done((f32[8,2048]{1,0:T(8,128)S(1)}, f32[8,2048]{1,0:T(8,128)S(1)}, u32[]{:S(2)}, u32[]{:S(2)}) %collective-permute-start.4) | collective-permute-done | bytes 65568 | tf_op jit(solution)/shard_map/ppermute | solution.py:316
  13.0 0.0 collective-permute-done.2
  13.0 0.0 collective-permute-done.3
  13.1 0.3 %collective-permute-start.6 = (f32[8,2048]{1,0:T(8,128)S(1)}, f32[8,2048]{1,0:T(8,128)S(1)}, u32[]{:S(2)}, u32[]{:S(2)}) collective-permute-start(f32[8,2048]{1,0:T(8,128)S(1)} %get-tuple-element.43), channel_id=1, source_target_pairs={{0,1},{1,0},{2,3},{3,2},{4,5},{5,4},{6,7},{7,6},{8,9},{9,8},{10,11... | collective-permute-start | bytes 196616 | tf_op jit(solution)/shard_map/ppermute | solution.py:323
  13.4 1.6 %local_filter.3.refs_2_ = f32[128,1024]{1,0:T(8,128)S(1)} custom-call(bf16[128,2048]{1,0:T(8,128)(2,1)S(1)} %copy-done.1, f32[128,2048]{1,0:T(8,128)S(1)} %get-tuple-element.36.driven.refs_1_, f32[16,2048]{1,0:T(8,128)S(1)} %copy-done, f32[16,2048]{1,0:T(8,128)S(1)} %copy-done.2, f32[1,2048]{1,0:T(1,128)S(1)} %bitcast.4), custom_call_target="tpu_custom_call" | custom-call | flops 8388608 | bytes 2367488 | tf_op jit(solution)/shard_map/local_filter/pallas_call | solution.py:224
  15.1 0.8 %add_kept.1.refs_1_ = f32[128,2048]{1,0:T(8,128)S(1)} custom-call(s32[1]{0:T(128)} %bitcast.refs_0_.x_ref, f32[128,1024]{1,0:T(8,128)S(1)} %local_filter.2.refs_1_, f32[128,1024]{1,0:T(8,128)S(1)} %local_filter.3.refs_2_, bf16[128,2048]{1,0:T(8,128)(2,1)S(1)} %copy-done.1, f32[8,2048]{1,0:T(8,128)S(1)} %add_select_fusion.2.refs_4_, f32[16,2048]{1,0:T(8,128)S(1)} %copy-done, ...), custom_call_target="tpu_custom_call" | custom-call | flops 4194304 | bytes 3080196 | tf_op jit(solution)/shard_map/add_kept/pallas_call | solution.py:224
  15.9 0.0 collective-permute-done.5
  15.9 0.4 %collective-permute-done.6 = f32[8,2048]{1,0:T(8,128)S(1)} collective-permute-done((f32[8,2048]{1,0:T(8,128)S(1)}, f32[8,2048]{1,0:T(8,128)S(1)}, u32[]{:S(2)}, u32[]{:S(2)}) %collective-permute-start.6) | collective-permute-done | bytes 65568 | tf_op jit(solution)/shard_map/ppermute | solution.py:323
  16.3 0.0 copy-start.4
  16.3 1.0 %add_received.1 = (f32[128,2048]{1,0:T(8,128)S(1)}, f32[1,128]{1,0:T(1,128)S(1)}) custom-call(s32[1]{0:T(128)} %bitcast.refs_0_.x_ref, f32[128,2048]{1,0:T(8,128)S(1)} %add_kept.1.refs_1_, bf16[128,2048]{1,0:T(8,128)(2,1)S(1)} %copy-done.1, f32[8,2048]{1,0:T(8,128)S(1)} %broadcast_select_fusion.refs_3_, f32[16,2048]{1,0:T(8,128)S(1)} %copy-done, ...), custom_call_target="tpu_custom_call" | custom-call | flops 4194304 | bytes 3080708 | tf_op jit(solution)/shard_map/add_received/pallas_call | solution.py:224
  17.3 2.6 %collective-permute-start.7 = (f32[1,128]{1,0:T(1,128)S(1)}, f32[1,128]{1,0:T(1,128)S(1)}, u32[]{:S(2)}, u32[]{:S(2)}) collective-permute-start(f32[1,128]{1,0:T(1,128)S(1)} %get-tuple-element.42), channel_id=1, source_target_pairs={{0,1},{1,0},{2,3},{3,2},{4,5},{5,4},{6,7},{7,6},{8,9},{9,8},{10,11... | collective-permute-start | bytes 1544 | tf_op jit(solution)/shard_map/ppermute | solution.py:392
  19.9 0.8 %collective-permute-done.7 = f32[1,128]{1,0:T(1,128)S(1)} collective-permute-done((f32[1,128]{1,0:T(1,128)S(1)}, f32[1,128]{1,0:T(1,128)S(1)}, u32[]{:S(2)}, u32[]{:S(2)}) %collective-permute-start.7) | collective-permute-done | bytes 544 | tf_op jit(solution)/shard_map/ppermute | solution.py:392
  20.7 0.4 %collective-permute-start.8 = (f32[1,128]{1,0:T(1,128)S(1)}, f32[1,128]{1,0:T(1,128)S(1)}, u32[]{:S(2)}, u32[]{:S(2)}) collective-permute-start(f32[1,128]{1,0:T(1,128)S(1)} %add.41.refs_2_), channel_id=1, source_target_pairs={{0,3},{1,2},{2,1},{3,0},{4,7},{5,6},{6,5},{7,4},{8,11},{9,10},{10,... | collective-permute-start | bytes 1544 | tf_op jit(solution)/shard_map/ppermute | solution.py:392
  21.1 2.6 %collective-permute-done.8.refs_3_ = f32[1,128]{1,0:T(1,128)S(1)} collective-permute-done((f32[1,128]{1,0:T(1,128)S(1)}, f32[1,128]{1,0:T(1,128)S(1)}, u32[]{:S(2)}, u32[]{:S(2)}) %collective-permute-start.8) | collective-permute-done | bytes 544 | tf_op jit(solution)/shard_map/ppermute | solution.py:392
  23.7 0.0 copy-done.4
  23.7 0.9 %norm.1 = bf16[128,2048]{1,0:T(8,128)(2,1)} custom-call(f32[128,2048]{1,0:T(8,128)S(1)} %get-tuple-element.41.refs_0_, f32[1,2048]{1,0:T(1,128)S(1)} %bitcast.5, f32[1,128]{1,0:T(1,128)S(1)} %add.41.refs_2_, f32[1,128]{1,0:T(1,128)S(1)} %collective-permute-done.8.refs_3_), custom_call_target="tpu_custom_call" | custom-call | flops 524288 | bytes 1582080 | tf_op jit(solution)/shard_map/norm/pallas_call | solution.py:224
  (11 shorter events, 0.2 us)
Async XLA Ops:
  0.0 2.3 %copy-start = (f32[16,2048]{1,0:T(8,128)S(1)}, f32[16,2048]{1,0:T(8,128)}, u32[]{:S(2)}) copy-start(f32[16,2048]{1,0:T(8,128)} %refs_4_) | copy-start | bytes 393220
  2.0 3.2 %collective-permute-start = (f32[8,2048]{1,0:T(8,128)S(1)}, f32[8,2048]{1,0:T(8,128)S(1)}, u32[]{:S(2)}, u32[]{:S(2)}) collective-permute-start(f32[8,2048]{1,0:T(8,128)S(1)} %get-tuple-element.24), channel_id=1, source_target_pairs={{0,4},{4,0},{8,12},{12,8},{16,20},{20,16},{24,28},{28,24},{1,5},{5... | collective-permute-start | bytes 196616 | tf_op jit(solution)/shard_map/ppermute | solution.py:267
  2.3 1.0 %copy-start.1 = (bf16[128,2048]{1,0:T(8,128)(2,1)S(1)}, bf16[128,2048]{1,0:T(8,128)(2,1)}, u32[]{:S(2)}) copy-start(bf16[128,2048]{1,0:T(8,128)(2,1)} %refs_2_.6) | copy-start | bytes 1572868
  2.3 1.1 %copy-start.2 = (f32[16,2048]{1,0:T(8,128)S(1)}, f32[16,2048]{1,0:T(8,128)}, u32[]{:S(2)}) copy-start(f32[16,2048]{1,0:T(8,128)} %refs_3_.6) | copy-start | bytes 393220
  2.3 1.1 %copy-start.3 = (f32[2048]{0:T(1024)S(1)}, f32[2048]{0:T(1024)}, u32[]{:S(2)}) copy-start(f32[2048]{0:T(1024)} %param.12) | copy-start | bytes 24580
  5.2 3.3 %collective-permute-start.1 = (f32[8,2048]{1,0:T(8,128)S(1)}, f32[8,2048]{1,0:T(8,128)S(1)}, u32[]{:S(2)}, u32[]{:S(2)}) collective-permute-start(f32[8,2048]{1,0:T(8,128)S(1)} %get-tuple-element.30), channel_id=1, source_target_pairs={{0,8},{1,9},{2,10},{3,11},{4,12},{5,13},{6,14},{7,15},{8,0},{9,1},... | collective-permute-start | bytes 196616 | tf_op jit(solution)/shard_map/ppermute | solution.py:316
  7.1 6.0 %collective-permute-start.2 = (f32[8,2048]{1,0:T(8,128)S(1)}, f32[8,2048]{1,0:T(8,128)S(1)}, u32[]{:S(2)}, u32[]{:S(2)}) collective-permute-start(f32[8,2048]{1,0:T(8,128)S(1)} %get-tuple-element.30), channel_id=1, source_target_pairs={{0,1},{1,0},{2,3},{3,2},{4,5},{5,4},{6,7},{7,6},{8,16},{9,17},{10,... | collective-permute-start | bytes 196616 | tf_op jit(solution)/shard_map/ppermute | solution.py:316
  7.2 5.9 %collective-permute-start.3 = (f32[8,2048]{1,0:T(8,128)S(1)}, f32[8,2048]{1,0:T(8,128)S(1)}, u32[]{:S(2)}, u32[]{:S(2)}) collective-permute-start(f32[8,2048]{1,0:T(8,128)S(1)} %get-tuple-element.30), channel_id=1, source_target_pairs={{0,16},{1,17},{2,18},{3,19},{4,20},{5,21},{6,22},{7,23},{8,0},{9,1... | collective-permute-start | bytes 196616 | tf_op jit(solution)/shard_map/ppermute | solution.py:316
  8.6 4.5 %collective-permute-start.4 = (f32[8,2048]{1,0:T(8,128)S(1)}, f32[8,2048]{1,0:T(8,128)S(1)}, u32[]{:S(2)}, u32[]{:S(2)}) collective-permute-start(f32[8,2048]{1,0:T(8,128)S(1)} %get-tuple-element.48), channel_id=1, source_target_pairs={{0,1},{1,0},{2,3},{3,2},{4,5},{5,4},{6,7},{7,6},{8,24},{9,25},{10,... | collective-permute-start | bytes 196616 | tf_op jit(solution)/shard_map/ppermute | solution.py:316
  8.8 7.1 %collective-permute-start.5 = (f32[8,2048]{1,0:T(8,128)S(1)}, f32[8,2048]{1,0:T(8,128)S(1)}, u32[]{:S(2)}, u32[]{:S(2)}) collective-permute-start(f32[8,2048]{1,0:T(8,128)S(1)} %get-tuple-element.40), channel_id=1, source_target_pairs={{0,4},{1,5},{2,6},{3,7},{4,0},{5,1},{6,2},{7,3},{8,12},{9,13},{10,... | collective-permute-start | bytes 196616 | tf_op jit(solution)/shard_map/ppermute | solution.py:323
  13.1 3.2 %collective-permute-start.6 = (f32[8,2048]{1,0:T(8,128)S(1)}, f32[8,2048]{1,0:T(8,128)S(1)}, u32[]{:S(2)}, u32[]{:S(2)}) collective-permute-start(f32[8,2048]{1,0:T(8,128)S(1)} %get-tuple-element.43), channel_id=1, source_target_pairs={{0,1},{1,0},{2,3},{3,2},{4,5},{5,4},{6,7},{7,6},{8,9},{9,8},{10,11... | collective-permute-start | bytes 196616 | tf_op jit(solution)/shard_map/ppermute | solution.py:323
  16.3 7.4 %copy-start.4 = (f32[2048]{0:T(1024)S(1)}, f32[2048]{0:T(1024)}, u32[]{:S(2)}) copy-start(f32[2048]{0:T(1024)} %param.13) | copy-start | bytes 24580
  17.3 3.4 %collective-permute-start.7 = (f32[1,128]{1,0:T(1,128)S(1)}, f32[1,128]{1,0:T(1,128)S(1)}, u32[]{:S(2)}, u32[]{:S(2)}) collective-permute-start(f32[1,128]{1,0:T(1,128)S(1)} %get-tuple-element.42), channel_id=1, source_target_pairs={{0,1},{1,0},{2,3},{3,2},{4,5},{5,4},{6,7},{7,6},{8,9},{9,8},{10,11... | collective-permute-start | bytes 1544 | tf_op jit(solution)/shard_map/ppermute | solution.py:392
  20.7 3.0 %collective-permute-start.8 = (f32[1,128]{1,0:T(1,128)S(1)}, f32[1,128]{1,0:T(1,128)S(1)}, u32[]{:S(2)}, u32[]{:S(2)}) collective-permute-start(f32[1,128]{1,0:T(1,128)S(1)} %add.41.refs_2_), channel_id=1, source_target_pairs={{0,3},{1,2},{2,1},{3,0},{4,7},{5,6},{6,5},{7,4},{8,11},{9,10},{10,... | collective-permute-start | bytes 1544 | tf_op jit(solution)/shard_map/ppermute | solution.py:392

commit v7 on v6

--- a/solution.py
+++ b/solution.py
@@ -114,7 +114,7 @@
             series[pl.ds(token * ROWS + i, ROWS, stride=ROWS), :] = driven[token:token + ROWS, at]
         return unused
 
-    lax.fori_loop(0, ROWS, spread, 0, unroll=2)
+    lax.fori_loop(0, ROWS, spread, 0, unroll=ROWS)
     decay = [decays[m * ROWS:(m + 1) * ROWS, :] for m in range(modes)]
     scale = [scales[m * ROWS:(m + 1) * ROWS, :] for m in range(modes)]
 
@@ -138,7 +138,7 @@
             )
         return unused
 
-    lax.fori_loop(0, ROWS, gate, 0, unroll=2)
+    lax.fori_loop(0, ROWS, gate, 0, unroll=ROWS)
 
 
 def carry_kernel(which, pieces, final, x_ref, *refs):
@@ -180,7 +180,7 @@
                     terms = [t * f for t, f in zip(terms, factors)]
             return unused
 
-        lax.fori_loop(0, groups, group_step, 0, unroll=4)
+        lax.fori_loop(0, groups, group_step, 0, unroll=groups)
     if final:
         squares[...] = jnp.sum(jnp.transpose(sums[...]), axis=0, keepdims=True)
 

time: 24.8 us -> 24.7 us (level)
  Pallas kernels: 8.8 us -> 8.28 us
  waiting for transfers between devices: 7.18 us -> 7.61 us
    pallas_call x9, Pallas kernels: 8.8 us -> 8.28 us  [call(): pl.pallas_call(kernel, out_shape=outputs, in_specs=specs, out_specs=out_s...]
    ppermute x2, waiting for transfers between devices: 0.4 us -> 0.66 us  [traded(): return lax.ppermute(array, ('ctx', 'tp'), links)]
  transfers between devices with their start and end apart: 9 -> 9, of which waited for: 5 -> 5; matrix products, arithmetic and copies ran while one was open for 0% -> 0% of each run, Pallas kernels for 20% -> 18%
where the time goes in v7:
time: 24.7 us; the launch traced here: 24.5 us
  Pallas kernels  8.28 us (34%)
  starting transfers between devices  8.14 us (33%)
  waiting for transfers between devices  7.61 us (31%)
  local copies, waits for them, and re-layouts  0.25 us (1%)
    pallas_call x9, Pallas kernels, call(): pl.pallas_call(kernel, out_shape=outputs, in_specs=specs, out_specs=out_s...  8.28 us
    ppermute x4, starting transfers between devices, moved(): return lax.ppermute(array, ('ctx', 'tp'), links)  3.51 us
    ppermute x2, waiting for transfers between devices, body(): lax.ppermute(parts[0], 'tp', [(i, i ^ mask) for i in range(tp)])  3.37 us
    ppermute x4, waiting for transfers between devices, moved(): return lax.ppermute(array, ('ctx', 'tp'), links)  3.23 us
    ppermute x2, starting transfers between devices, body(): lax.ppermute(parts[0], 'tp', [(i, i ^ mask) for i in range(tp)])  3.02 us
    ppermute x2, starting transfers between devices, traded(): return lax.ppermute(array, ('ctx', 'tp'), links)  1.29 us
    ppermute x2, waiting for transfers between devices, traded(): return lax.ppermute(array, ('ctx', 'tp'), links)  0.66 us
  transfers between devices with their start and end apart: 9, of which 5 were waited for; matrix products, arithmetic and copies ran while one was open for 0% of the time, Pallas kernels for 18%

profile of v7, /device:TPU:31, one launch (start us, length us, event | category | flops | bytes accessed | tf_op | source)
XLA Modules:
  0.0 24.5 jit_solution(3079561388531485729)
XLA Ops:
  0.0 2.0 %first_ends.1 = (f32[8,2048]{1,0:T(8,128)S(1)}, f32[128,2048]{1,0:T(8,128)S(1)}) custom-call(s32[1]{0:T(128)} %bitcast.refs_0_.x_ref, bf16[128,2048]{1,0:T(8,128)(2,1)} %refs_1_.1, bf16[128,2048]{1,0:T(8,128)(2,1)} %refs_2_.3, f32[16,2048]{1,0:T(8,128)} %refs_4_), custom_call_target="tpu_custom_call" | custom-call | flops 4194304 | bytes 2293764 | tf_op jit(solution)/shard_map/first_ends/pallas_call | solution.py:224
  2.0 0.3 %collective-permute-start = (f32[8,2048]{1,0:T(8,128)S(1)}, f32[8,2048]{1,0:T(8,128)S(1)}, u32[]{:S(2)}, u32[]{:S(2)}) collective-permute-start(f32[8,2048]{1,0:T(8,128)S(1)} %get-tuple-element.24), channel_id=1, source_target_pairs={{0,4},{4,0},{8,12},{12,8},{16,20},{20,16},{24,28},{28,24},{1,5},{5... | collective-permute-start | bytes 196616 | tf_op jit(solution)/shard_map/ppermute | solution.py:267
  2.3 0.0 copy-done
  2.3 0.8 %second_ends.1 = f32[8,2048]{1,0:T(8,128)S(1)} custom-call(s32[1]{0:T(128)} %bitcast.refs_0_.x_ref, f32[128,2048]{1,0:T(8,128)S(1)} %get-tuple-element.36.driven.refs_1_, f32[16,2048]{1,0:T(8,128)S(1)} %copy-done), custom_call_target="tpu_custom_call" | custom-call | flops 4194304 | bytes 1245188 | tf_op jit(solution)/shard_map/second_ends/pallas_call | solution.py:224
  3.1 0.2 copy-done.1
  3.3 0.0 copy-done.2
  3.4 0.0 copy-done.3
  3.4 1.4 %local_filter.2.refs_1_ = f32[128,1024]{1,0:T(8,128)S(1)} custom-call(bf16[128,2048]{1,0:T(8,128)(2,1)S(1)} %copy-done.1, f32[128,2048]{1,0:T(8,128)S(1)} %get-tuple-element.36.driven.refs_1_, f32[16,2048]{1,0:T(8,128)S(1)} %copy-done, f32[16,2048]{1,0:T(8,128)S(1)} %copy-done.2, f32[1,2048]{1,0:T(1,128)S(1)} %bitcast.3), custom_call_target="tpu_custom_call" | custom-call | flops 8388608 | bytes 2367488 | tf_op jit(solution)/shard_map/local_filter/pallas_call | solution.py:224
  4.8 0.3 %collective-permute-done = f32[8,2048]{1,0:T(8,128)S(1)} collective-permute-done((f32[8,2048]{1,0:T(8,128)S(1)}, f32[8,2048]{1,0:T(8,128)S(1)}, u32[]{:S(2)}, u32[]{:S(2)}) %collective-permute-start) | collective-permute-done | bytes 65568 | tf_op jit(solution)/shard_map/ppermute | solution.py:267
  5.2 1.9 %collective-permute-start.1 = (f32[8,2048]{1,0:T(8,128)S(1)}, f32[8,2048]{1,0:T(8,128)S(1)}, u32[]{:S(2)}, u32[]{:S(2)}) collective-permute-start(f32[8,2048]{1,0:T(8,128)S(1)} %get-tuple-element.30), channel_id=1, source_target_pairs={{0,8},{1,9},{2,10},{3,11},{4,12},{5,13},{6,14},{7,15},{8,0},{9,1},... | collective-permute-start | bytes 196616 | tf_op jit(solution)/shard_map/ppermute | solution.py:316
  7.1 0.1 collective-permute-start.2
  7.2 1.3 %collective-permute-start.3 = (f32[8,2048]{1,0:T(8,128)S(1)}, f32[8,2048]{1,0:T(8,128)S(1)}, u32[]{:S(2)}, u32[]{:S(2)}) collective-permute-start(f32[8,2048]{1,0:T(8,128)S(1)} %get-tuple-element.30), channel_id=1, source_target_pairs={{0,16},{1,17},{2,18},{3,19},{4,20},{5,21},{6,22},{7,23},{8,0},{9,1... | collective-permute-start | bytes 196616 | tf_op jit(solution)/shard_map/ppermute | solution.py:316
  8.5 0.1 scales.1.refs_6_.refs_5_
  8.5 0.0 collective-permute-done.1
  8.6 0.2 %collective-permute-start.4 = (f32[8,2048]{1,0:T(8,128)S(1)}, f32[8,2048]{1,0:T(8,128)S(1)}, u32[]{:S(2)}, u32[]{:S(2)}) collective-permute-start(f32[8,2048]{1,0:T(8,128)S(1)} %get-tuple-element.48), channel_id=1, source_target_pairs={{0,1},{1,0},{2,3},{3,2},{4,5},{5,4},{6,7},{7,6},{8,24},{9,25},{10,... | collective-permute-start | bytes 196616 | tf_op jit(solution)/shard_map/ppermute | solution.py:316
  8.8 1.0 %collective-permute-start.5 = (f32[8,2048]{1,0:T(8,128)S(1)}, f32[8,2048]{1,0:T(8,128)S(1)}, u32[]{:S(2)}, u32[]{:S(2)}) collective-permute-start(f32[8,2048]{1,0:T(8,128)S(1)} %get-tuple-element.40), channel_id=1, source_target_pairs={{0,4},{1,5},{2,6},{3,7},{4,0},{5,1},{6,2},{7,3},{8,12},{9,13},{10,... | collective-permute-start | bytes 196616 | tf_op jit(solution)/shard_map/ppermute | solution.py:323
  9.8 3.2 %collective-permute-done.4 = f32[8,2048]{1,0:T(8,128)S(1)} collective-permute-done((f32[8,2048]{1,0:T(8,128)S(1)}, f32[8,2048]{1,0:T(8,128)S(1)}, u32[]{:S(2)}, u32[]{:S(2)}) %collective-permute-start.4) | collective-permute-done | bytes 65568 | tf_op jit(solution)/shard_map/ppermute | solution.py:316
  13.0 0.0 collective-permute-done.2
  13.0 0.0 collective-permute-done.3
  13.1 0.3 %collective-permute-start.6 = (f32[8,2048]{1,0:T(8,128)S(1)}, f32[8,2048]{1,0:T(8,128)S(1)}, u32[]{:S(2)}, u32[]{:S(2)}) collective-permute-start(f32[8,2048]{1,0:T(8,128)S(1)} %get-tuple-element.43), channel_id=1, source_target_pairs={{0,1},{1,0},{2,3},{3,2},{4,5},{5,4},{6,7},{7,6},{8,9},{9,8},{10,11... | collective-permute-start | bytes 196616 | tf_op jit(solution)/shard_map/ppermute | solution.py:323
  13.4 1.4 %local_filter.3.refs_2_ = f32[128,1024]{1,0:T(8,128)S(1)} custom-call(bf16[128,2048]{1,0:T(8,128)(2,1)S(1)} %copy-done.1, f32[128,2048]{1,0:T(8,128)S(1)} %get-tuple-element.36.driven.refs_1_, f32[16,2048]{1,0:T(8,128)S(1)} %copy-done, f32[16,2048]{1,0:T(8,128)S(1)} %copy-done.2, f32[1,2048]{1,0:T(1,128)S(1)} %bitcast.4), custom_call_target="tpu_custom_call" | custom-call | flops 8388608 | bytes 2367488 | tf_op jit(solution)/shard_map/local_filter/pallas_call | solution.py:224
  14.9 0.7 %add_kept.1.refs_1_ = f32[128,2048]{1,0:T(8,128)S(1)} custom-call(s32[1]{0:T(128)} %bitcast.refs_0_.x_ref, f32[128,1024]{1,0:T(8,128)S(1)} %local_filter.2.refs_1_, f32[128,1024]{1,0:T(8,128)S(1)} %local_filter.3.refs_2_, bf16[128,2048]{1,0:T(8,128)(2,1)S(1)} %copy-done.1, f32[8,2048]{1,0:T(8,128)S(1)} %add_select_fusion.2.refs_4_, f32[16,2048]{1,0:T(8,128)S(1)} %copy-done, ...), custom_call_target="tpu_custom_call" | custom-call | flops 4194304 | bytes 3080196 | tf_op jit(solution)/shard_map/add_kept/pallas_call | solution.py:224
  15.6 0.0 collective-permute-done.5
  15.6 0.7 %collective-permute-done.6 = f32[8,2048]{1,0:T(8,128)S(1)} collective-permute-done((f32[8,2048]{1,0:T(8,128)S(1)}, f32[8,2048]{1,0:T(8,128)S(1)}, u32[]{:S(2)}, u32[]{:S(2)}) %collective-permute-start.6) | collective-permute-done | bytes 65568 | tf_op jit(solution)/shard_map/ppermute | solution.py:323
  16.3 0.0 copy-start.4
  16.3 0.9 %add_received.1 = (f32[128,2048]{1,0:T(8,128)S(1)}, f32[1,128]{1,0:T(1,128)S(1)}) custom-call(s32[1]{0:T(128)} %bitcast.refs_0_.x_ref, f32[128,2048]{1,0:T(8,128)S(1)} %add_kept.1.refs_1_, bf16[128,2048]{1,0:T(8,128)(2,1)S(1)} %copy-done.1, f32[8,2048]{1,0:T(8,128)S(1)} %broadcast_select_fusion.refs_3_, f32[16,2048]{1,0:T(8,128)S(1)} %copy-done, ...), custom_call_target="tpu_custom_call" | custom-call | flops 4194304 | bytes 3080708 | tf_op jit(solution)/shard_map/add_received/pallas_call | solution.py:224
  17.2 2.6 %collective-permute-start.7 = (f32[1,128]{1,0:T(1,128)S(1)}, f32[1,128]{1,0:T(1,128)S(1)}, u32[]{:S(2)}, u32[]{:S(2)}) collective-permute-start(f32[1,128]{1,0:T(1,128)S(1)} %get-tuple-element.42), channel_id=1, source_target_pairs={{0,1},{1,0},{2,3},{3,2},{4,5},{5,4},{6,7},{7,6},{8,9},{9,8},{10,11... | collective-permute-start | bytes 1544 | tf_op jit(solution)/shard_map/ppermute | solution.py:392
  19.8 0.8 %collective-permute-done.7 = f32[1,128]{1,0:T(1,128)S(1)} collective-permute-done((f32[1,128]{1,0:T(1,128)S(1)}, f32[1,128]{1,0:T(1,128)S(1)}, u32[]{:S(2)}, u32[]{:S(2)}) %collective-permute-start.7) | collective-permute-done | bytes 544 | tf_op jit(solution)/shard_map/ppermute | solution.py:392
  20.6 0.4 %collective-permute-start.8 = (f32[1,128]{1,0:T(1,128)S(1)}, f32[1,128]{1,0:T(1,128)S(1)}, u32[]{:S(2)}, u32[]{:S(2)}) collective-permute-start(f32[1,128]{1,0:T(1,128)S(1)} %add.41.refs_2_), channel_id=1, source_target_pairs={{0,3},{1,2},{2,1},{3,0},{4,7},{5,6},{6,5},{7,4},{8,11},{9,10},{10,... | collective-permute-start | bytes 1544 | tf_op jit(solution)/shard_map/ppermute | solution.py:392
  21.0 2.6 %collective-permute-done.8.refs_3_ = f32[1,128]{1,0:T(1,128)S(1)} collective-permute-done((f32[1,128]{1,0:T(1,128)S(1)}, f32[1,128]{1,0:T(1,128)S(1)}, u32[]{:S(2)}, u32[]{:S(2)}) %collective-permute-start.8) | collective-permute-done | bytes 544 | tf_op jit(solution)/shard_map/ppermute | solution.py:392
  23.6 0.0 copy-done.4
  23.6 0.9 %norm.1 = bf16[128,2048]{1,0:T(8,128)(2,1)} custom-call(f32[128,2048]{1,0:T(8,128)S(1)} %get-tuple-element.41.refs_0_, f32[1,2048]{1,0:T(1,128)S(1)} %bitcast.5, f32[1,128]{1,0:T(1,128)S(1)} %add.41.refs_2_, f32[1,128]{1,0:T(1,128)S(1)} %collective-permute-done.8.refs_3_), custom_call_target="tpu_custom_call" | custom-call | flops 524288 | bytes 1582080 | tf_op jit(solution)/shard_map/norm/pallas_call | solution.py:224
  (11 shorter events, 0.2 us)
Async XLA Ops:
  0.0 2.3 %copy-start = (f32[16,2048]{1,0:T(8,128)S(1)}, f32[16,2048]{1,0:T(8,128)}, u32[]{:S(2)}) copy-start(f32[16,2048]{1,0:T(8,128)} %refs_4_) | copy-start | bytes 393220
  2.0 3.2 %collective-permute-start = (f32[8,2048]{1,0:T(8,128)S(1)}, f32[8,2048]{1,0:T(8,128)S(1)}, u32[]{:S(2)}, u32[]{:S(2)}) collective-permute-start(f32[8,2048]{1,0:T(8,128)S(1)} %get-tuple-element.24), channel_id=1, source_target_pairs={{0,4},{4,0},{8,12},{12,8},{16,20},{20,16},{24,28},{28,24},{1,5},{5... | collective-permute-start | bytes 196616 | tf_op jit(solution)/shard_map/ppermute | solution.py:267
  2.3 1.0 %copy-start.1 = (bf16[128,2048]{1,0:T(8,128)(2,1)S(1)}, bf16[128,2048]{1,0:T(8,128)(2,1)}, u32[]{:S(2)}) copy-start(bf16[128,2048]{1,0:T(8,128)(2,1)} %refs_2_.6) | copy-start | bytes 1572868
  2.3 1.1 %copy-start.2 = (f32[16,2048]{1,0:T(8,128)S(1)}, f32[16,2048]{1,0:T(8,128)}, u32[]{:S(2)}) copy-start(f32[16,2048]{1,0:T(8,128)} %refs_3_.6) | copy-start | bytes 393220
  2.3 1.1 %copy-start.3 = (f32[2048]{0:T(1024)S(1)}, f32[2048]{0:T(1024)}, u32[]{:S(2)}) copy-start(f32[2048]{0:T(1024)} %param.12) | copy-start | bytes 24580
  5.2 3.3 %collective-permute-start.1 = (f32[8,2048]{1,0:T(8,128)S(1)}, f32[8,2048]{1,0:T(8,128)S(1)}, u32[]{:S(2)}, u32[]{:S(2)}) collective-permute-start(f32[8,2048]{1,0:T(8,128)S(1)} %get-tuple-element.30), channel_id=1, source_target_pairs={{0,8},{1,9},{2,10},{3,11},{4,12},{5,13},{6,14},{7,15},{8,0},{9,1},... | collective-permute-start | bytes 196616 | tf_op jit(solution)/shard_map/ppermute | solution.py:316
  7.1 6.0 %collective-permute-start.2 = (f32[8,2048]{1,0:T(8,128)S(1)}, f32[8,2048]{1,0:T(8,128)S(1)}, u32[]{:S(2)}, u32[]{:S(2)}) collective-permute-start(f32[8,2048]{1,0:T(8,128)S(1)} %get-tuple-element.30), channel_id=1, source_target_pairs={{0,1},{1,0},{2,3},{3,2},{4,5},{5,4},{6,7},{7,6},{8,16},{9,17},{10,... | collective-permute-start | bytes 196616 | tf_op jit(solution)/shard_map/ppermute | solution.py:316
  7.2 5.9 %collective-permute-start.3 = (f32[8,2048]{1,0:T(8,128)S(1)}, f32[8,2048]{1,0:T(8,128)S(1)}, u32[]{:S(2)}, u32[]{:S(2)}) collective-permute-start(f32[8,2048]{1,0:T(8,128)S(1)} %get-tuple-element.30), channel_id=1, source_target_pairs={{0,16},{1,17},{2,18},{3,19},{4,20},{5,21},{6,22},{7,23},{8,0},{9,1... | collective-permute-start | bytes 196616 | tf_op jit(solution)/shard_map/ppermute | solution.py:316
  8.6 4.5 %collective-permute-start.4 = (f32[8,2048]{1,0:T(8,128)S(1)}, f32[8,2048]{1,0:T(8,128)S(1)}, u32[]{:S(2)}, u32[]{:S(2)}) collective-permute-start(f32[8,2048]{1,0:T(8,128)S(1)} %get-tuple-element.48), channel_id=1, source_target_pairs={{0,1},{1,0},{2,3},{3,2},{4,5},{5,4},{6,7},{7,6},{8,24},{9,25},{10,... | collective-permute-start | bytes 196616 | tf_op jit(solution)/shard_map/ppermute | solution.py:316
  8.8 6.8 %collective-permute-start.5 = (f32[8,2048]{1,0:T(8,128)S(1)}, f32[8,2048]{1,0:T(8,128)S(1)}, u32[]{:S(2)}, u32[]{:S(2)}) collective-permute-start(f32[8,2048]{1,0:T(8,128)S(1)} %get-tuple-element.40), channel_id=1, source_target_pairs={{0,4},{1,5},{2,6},{3,7},{4,0},{5,1},{6,2},{7,3},{8,12},{9,13},{10,... | collective-permute-start | bytes 196616 | tf_op jit(solution)/shard_map/ppermute | solution.py:323
  13.1 3.2 %collective-permute-start.6 = (f32[8,2048]{1,0:T(8,128)S(1)}, f32[8,2048]{1,0:T(8,128)S(1)}, u32[]{:S(2)}, u32[]{:S(2)}) collective-permute-start(f32[8,2048]{1,0:T(8,128)S(1)} %get-tuple-element.43), channel_id=1, source_target_pairs={{0,1},{1,0},{2,3},{3,2},{4,5},{5,4},{6,7},{7,6},{8,9},{9,8},{10,11... | collective-permute-start | bytes 196616 | tf_op jit(solution)/shard_map/ppermute | solution.py:323
  16.3 7.3 %copy-start.4 = (f32[2048]{0:T(1024)S(1)}, f32[2048]{0:T(1024)}, u32[]{:S(2)}) copy-start(f32[2048]{0:T(1024)} %param.13) | copy-start | bytes 24580
  17.2 3.4 %collective-permute-start.7 = (f32[1,128]{1,0:T(1,128)S(1)}, f32[1,128]{1,0:T(1,128)S(1)}, u32[]{:S(2)}, u32[]{:S(2)}) collective-permute-start(f32[1,128]{1,0:T(1,128)S(1)} %get-tuple-element.42), channel_id=1, source_target_pairs={{0,1},{1,0},{2,3},{3,2},{4,5},{5,4},{6,7},{7,6},{8,9},{9,8},{10,11... | collective-permute-start | bytes 1544 | tf_op jit(solution)/shard_map/ppermute | solution.py:392
  20.6 3.0 %collective-permute-start.8 = (f32[1,128]{1,0:T(1,128)S(1)}, f32[1,128]{1,0:T(1,128)S(1)}, u32[]{:S(2)}, u32[]{:S(2)}) collective-permute-start(f32[1,128]{1,0:T(1,128)S(1)} %add.41.refs_2_), channel_id=1, source_target_pairs={{0,3},{1,2},{2,1},{3,0},{4,7},{5,6},{6,5},{7,4},{8,11},{9,10},{10,... | collective-permute-start | bytes 1544 | tf_op jit(solution)/shard_map/ppermute | solution.py:392
